TPU v7x, 32 devices: a whole 2x2x4 slice. The times are simulated.
32 devices in a mesh: dp: 8 (over z, x), vocab: 4 (over y, core).
Axes of the slice: x: 2, y: 2, z: 4, core: 2. Of those that a mesh axis runs over, the one named last changes fastest.
Arguments:
- hidden: bfloat16 [512, 4096], P('dp', 'vocab'), may hold values from -400 to 400
- output_head_matrix: bfloat16 [4096, 151936], P(None, ('dp', 'vocab')), may hold values from -0.09375 to 0.09375
- row_counts: int32 [8], replicated, may hold values from 1 to 64, 256 in all
- token_ids: int32 [256], P('dp'), may hold values from 0 to 151935
- segment_ids: int32 [256], P('dp'), may hold values from 0 to 15, never falling along the last dimension, each value on 1 to 64 neighbouring positions
- cotangent: float32 [256], P('dp'), may hold values from -6 to 6
Outputs:
- logprobs: float32 [256], P('dp')
- grad_hidden: bfloat16 [512, 4096], P('dp', 'vocab')
Inputs may be any that keep to these rules, and one draw needn't show every extreme that they name: `row_counts`: live rows of each index of dp; they sum to 256, one index holds 64. `segment_ids`: never falling; each segment has 1 to 64 positions, one exactly 64.
All inputs are finite; a program needn't handle non-finite values.
Results may differ from a plain program's by a relative error of at most 0.0034.
Values may be sent and summed in bfloat16 or wider, within the bound.
A program may use at most 128 MiB of HBM per device.

v0:
```python
import jax
import jax.numpy as jnp
from jax import lax
from jax.sharding import PartitionSpec as P

freq_weight = 0.4
presence_weight = 0.8


def per_device(hidden, output_head_matrix, row_counts, token_ids, segment_ids, cotangent):
    dp_count = lax.axis_size("dp")
    voc_count = lax.axis_size("vocab")
    dp_index = lax.axis_index("dp")
    slot_rows, feat_cols = hidden.shape
    per_peer = slot_rows // dp_count
    tok_rows = token_ids.shape[0]
    total_rows = tok_rows * dp_count
    voc_cols = output_head_matrix.shape[1]
    ends = jnp.cumsum(row_counts)
    starts = ends - row_counts
    my_start = starts[dp_index]
    live = jnp.arange(slot_rows, dtype=jnp.int32) < row_counts[dp_index]
    outgoing = jnp.where(live[:, None], hidden, jnp.zeros_like(hidden))
    outgoing = jnp.roll(outgoing.reshape(per_peer, dp_count, feat_cols), my_start, axis=1)
    arrived = lax.all_to_all(outgoing, "dp", split_axis=1, concat_axis=1, tiled=True)
    offsets = jnp.mod(dp_index - starts, dp_count)
    base_pos = (starts + offsets - dp_index) // dp_count
    turns = jnp.arange(per_peer, dtype=jnp.int32)[:, None]
    valid = turns * dp_count + offsets[None, :] < row_counts[None, :]
    target_position = (base_pos[None, :] + turns).reshape(-1)
    placing = (
        target_position[None, :] == jnp.arange(tok_rows, dtype=jnp.int32)[:, None]
    ) & valid.reshape(-1)[None, :]
    placing = placing.astype(jnp.bfloat16)
    packed = jnp.dot(
        placing, arrived.reshape(per_peer * dp_count, feat_cols), preferred_element_type=jnp.float32
    ).astype(jnp.bfloat16)
    gathered_token_ids, segs_all = (
        lax.all_gather(token_ids, "dp", axis=0, tiled=True),
        lax.all_gather(segment_ids, "dp", axis=0, tiled=True),
    )
    gathered_hidden_rows = lax.all_gather(packed, "dp", axis=0, tiled=True)
    logits = jnp.dot(
        lax.all_gather(gathered_hidden_rows, "vocab", axis=1, tiled=True),
        output_head_matrix,
        preferred_element_type=jnp.float32,
    )
    col_start = (dp_index * voc_count + lax.axis_index("vocab")) * voc_cols
    columns = col_start + jnp.arange(voc_cols, dtype=jnp.int32)
    hits = gathered_token_ids[:, None] == columns[None, :]
    positions = jnp.arange(total_rows, dtype=jnp.int32)
    prior_token_hits = (segs_all[:, None] == segs_all[None, :]) & (
        positions[None, :] < positions[:, None]
    )
    counts = jnp.dot(
        prior_token_hits.astype(jnp.bfloat16),
        hits.astype(jnp.bfloat16),
        preferred_element_type=jnp.float32,
    )
    scores = logits - freq_weight * counts - presence_weight * (counts > 0).astype(jnp.float32)
    picked_local = jnp.sum(jnp.where(hits, scores, jnp.zeros_like(scores)), axis=1)
    top = lax.pmax(jnp.max(scores, axis=1), ("dp", "vocab"))
    shifted = jnp.exp(scores - top[:, None])
    total, picked = lax.psum((jnp.sum(shifted, axis=1), picked_local), ("dp", "vocab"))
    all_logprobs = picked - top - jnp.log(total)
    logprobs = lax.dynamic_slice_in_dim(all_logprobs, dp_index * tok_rows, tok_rows, 0)
    residual = (hits.astype(jnp.float32) - shifted / total[:, None]).astype(jnp.bfloat16)
    head_weight_tiles = output_head_matrix.reshape(voc_count, feat_cols, voc_cols)
    blocks = tok_rows * lax.axis_size(("dp", "vocab")) // tok_rows
    span = min(dp_count, blocks // voc_count + 2)
    local_hidden_rows = residual
    local_hidden_rows = local_hidden_rows.reshape(span, tok_rows, voc_cols)
    product = jnp.einsum(
        "ubw,axw->uabx", local_hidden_rows, head_weight_tiles, preferred_element_type=jnp.float32
    )
    product = product.reshape(span * voc_count * tok_rows, feat_cols)
    summed = lax.psum_scatter(product, ("dp", "vocab"), scatter_dimension=0, tiled=True)
    scaled = (summed * cotangent[:, None]).astype(jnp.bfloat16)
    sending = jnp.dot(placing.T, scaled, preferred_element_type=jnp.float32).astype(jnp.bfloat16)
    sending = sending.reshape(per_peer, dp_count, feat_cols)
    returned = lax.all_to_all(sending, "dp", split_axis=1, concat_axis=1, tiled=True)
    grad_hidden = jnp.roll(returned, -my_start, axis=1).reshape(slot_rows, feat_cols)
    return (logprobs, grad_hidden)


def solution(mesh):
    return jax.shard_map(
        per_device,
        mesh=mesh,
        in_specs=(P("dp", "vocab"), P(None, ("dp", "vocab")), P(), P("dp"), P("dp"), P("dp")),
        out_specs=(P("dp"), P("dp", "vocab")),
        check_vma=False,
    )
```

profile of v0, /device:TPU:0, one launch (start us, length us, event | category | flops | bytes accessed | tf_op | source)
XLA Modules:
  0.0 450.1 jit_solution(1031778776090014118)
XLA Ops:
  7.2 1.2 dynamic_slice.12
  8.4 0.6 iota_compare_fusion.2
  9.1 0.8 reduce-window.9
  9.9 0.7 and_select_fusion
  10.6 0.7 dynamic_slice.13
  13.3 1.0 select_bitcast_fusion
  14.3 0.1 fusion.18
  14.5 0.7 copy.15
  15.2 7.3 %all-to-all-start = ((bf16[8,8,1024]{2,0,1:T(8,128)(2,1)}), bf16[8,8,1024]{2,0,1:T(8,128)(2,1)S(1)}, u32[]{:S(2)}, u32[]{:S(2)}) async-start(bf16[8,8,1024]{2,0,1:T(8,128)(2,1)} %copy.15), calls=%async_computation | async-start | bytes 262144 | tf_op jit(solution)/shard_map/all_to_all | solution.py:25
  22.4 0.0 all-gather.2.cloned.1.call-start
  22.5 0.7 add_compare_fusion
  23.2 0.1 lt.63
  23.3 0.1 add.90
  23.4 6.4 %all-to-all-done = bf16[8,8,1024]{2,0,1:T(8,128)(2,1)S(1)} async-done(((bf16[8,8,1024]{2,0,1:T(8,128)(2,1)}), bf16[8,8,1024]{2,0,1:T(8,128)(2,1)S(1)}, u32[]{:S(2)}, u32[]{:S(2)}) %all-to-all-start) | async-done | bytes 131104 | tf_op jit(solution)/shard_map/all_to_all | solution.py:25
  29.8 0.2 convolution_convert_fusion.1
  30.0 33.5 %all_gather.13 = bf16[256,1024]{1,0:T(8,128)(2,1)} all-gather(bf16[32,1024]{1,0:T(8,128)(2,1)S(1)} %convolution_convert_fusion.1), channel_id=1, replica_groups=mesh['dp'=8,'vocab'=4] {'dp'}, dimensions={0}, use_global_device_ids=true | all-gather | bytes 589824 | tf_op jit(solution)/shard_map/all_gather | solution.py:42
  63.5 0.0 all-gather.2.cloned.1.call-update
  63.6 0.0 reduce-scatter.2.cloned.1.call-start
  63.6 0.0 copy-start.3
  63.6 0.0 copy-start.1
  63.6 0.0 copy-start.2
  63.7 78.7 %reshape.114 = bf16[4,1024,4748]{1,0,2:T(4,128)(2,1)} reshape(bf16[4096,4748]{0,1:T(8,128)(2,1)} %param.9) | data formatting | bytes 77791232 | tf_op jit(solution)/shard_map/reshape | solution.py:68
  142.3 0.0 copy-done.3
  142.3 0.6 dynamic-slice
  143.6 0.0 copy-done.1
  143.6 0.2 dynamic-update-slice
  143.8 0.0 copy-done.2
  143.8 0.2 dynamic-update-slice.1
  144.1 8.5 %all-reduce.2 = (s32[256]{0:T(256)S(1)}, s32[256]{0:T(256)S(1)}) all-reduce(s32[256]{0:T(256)S(1)} %dynamic-update-slice, s32[256]{0:T(256)S(1)} %dynamic-update-slice.1), channel_id=1, replica_groups=mesh['dp'=8,'vocab'=4] {'dp'}, use_global_device_ids=true, to_apply=%add | all-reduce | flops 512 | bytes 4096
  152.6 3.7 fusion.3
  156.3 0.0 all-gather.2.cloned.1.call-done
  156.3 21.0 %fusion.32 = (f32[256]{0:T(256)S(1)}, f32[256,4748]{0,1:T(8,128)}) fusion(f32[256,4748]{0,1:T(8,128)} %fusion.3, bf16[256,4096]{1,0:T(8,128)(2,1)} %all-gather.2.cloned.1.call-done, bf16[4096,4748]{0,1:T(8,128)(2,1)} %param.9), kind=kOutput, calls=%fused_computation.57 | convolution fusion | flops 9964570624 | bytes 50717696 | tf_op jit(solution)/shard_map/dot_general | solution.py:43
  177.3 38.6 %pmax.7 = f32[256]{0:T(256)S(1)} all-reduce(f32[256]{0:T(256)S(1)} %get-tuple-element.12), channel_id=1, replica_groups=mesh['dp'=8,'vocab'=4] {'dp','vocab'}, use_global_device_ids=true, to_apply=%region_4.6 | all-reduce | flops 256 | bytes 2048 | tf_op jit(solution)/shard_map/pmax | solution.py:62
  216.0 4.3 fusion.6
  220.2 41.8 %all-reduce.3 = (f32[256]{0:T(256)S(1)}, f32[256]{0:T(256)S(1)}) all-reduce(f32[256]{0:T(256)S(1)} %get-tuple-element.4, f32[256]{0:T(256)S(1)} %get-tuple-element.3), channel_id=1, replica_groups=mesh['dp'=8,'vocab'=4] {'dp','vocab'}, use_global_device_ids=true, to_apply=%region_6.8 | all-reduce | flops 512 | bytes 4096 | tf_op jit(solution)/shard_map/psum | solution.py:64
  262.0 4.2 fusion.8
  266.2 3.6 copy.17
  269.8 0.0 copy-start
  269.8 19.2 %fusion = f32[8,32,4,1024]{3,1,2,0:T(8,128)} fusion(bf16[8,32,4748,1]{2,1,3,0:T(8,128)(2,1)} %bitcast.33, bf16[4,1024,4748]{1,0,2:T(4,128)(2,1)} %reshape.114), kind=kOutput, calls=%fused_computation | convolution fusion | flops 9957277696 | bytes 45520896 | tf_op jit(solution)/shard_map/ubw,axw->uabx/dot_general | solution.py:73
  289.1 0.0 reduce-scatter.2.cloned.1.call-update
  289.1 140.7 %reduce-scatter.2.cloned.1.call-done = f32[32,1024]{1,0:T(8,128)} async-done(((f32[1024,1024]{1,0:T(8,128)}), f32[32,1024]{1,0:T(8,128)}) %reduce-scatter.2.cloned.1.call-update) | async-done | bytes 131088 | tf_op jit(solution)/shard_map/reduce_scatter | solution.py:77
  429.8 0.0 copy-done
  429.8 1.1 fusion.12
  431.0 0.7 copy.19
  431.7 3.4 all-to-all-start.1
  435.8 0.6 dynamic_slice.14
  436.4 6.0 %all-to-all-done.1 = bf16[8,8,1024]{2,0,1:T(8,128)(2,1)S(1)} async-done(((bf16[8,8,1024]{2,0,1:T(8,128)(2,1)}), bf16[8,8,1024]{2,0,1:T(8,128)(2,1)S(1)}, u32[]{:S(2)}, u32[]{:S(2)}) %all-to-all-start.1) | async-done | bytes 131104 | tf_op jit(solution)/shard_map/all_to_all | solution.py:81
  442.4 0.1 copy.20
  442.5 0.8 fusion.17
  (6 shorter events, 0.0 us)
Async XLA Ops:
  15.2 14.6 %all-to-all-start = ((bf16[8,8,1024]{2,0,1:T(8,128)(2,1)}), bf16[8,8,1024]{2,0,1:T(8,128)(2,1)S(1)}, u32[]{:S(2)}, u32[]{:S(2)}) async-start(bf16[8,8,1024]{2,0,1:T(8,128)(2,1)} %copy.15), calls=%async_computation | async-start | bytes 262144 | tf_op jit(solution)/shard_map/all_to_all | solution.py:25
  22.4 133.9 %all-gather.2.cloned.1.call-start = ((), (), s32[]{:S(2)}) async-start(), calls=%async_computation.3 | async-start | bytes 2621440 | tf_op jit(solution)/shard_map/all_gather | solution.py:44
  63.6 366.3 %reduce-scatter.2.cloned.1.call-start = ((), (), s32[]{:S(2)}) async-start(), calls=%async_computation.4 | async-start | bytes 4325376 | tf_op jit(solution)/shard_map/reduce_scatter | solution.py:77
  63.6 78.7 %copy-start.3 = (u32[32]{0:T(128)S(1)}, u32[32]{0:T(128)}, u32[]{:S(2)}) copy-start(u32[32]{0:T(128)} %constant.82) | copy-start | bytes 388
  63.6 80.0 %copy-start.1 = (s32[32]{0:T(128)S(1)}, s32[32]{0:T(128)}, u32[]{:S(2)}) copy-start(s32[32]{0:T(128)} %param.11) | copy-start | bytes 388
  63.6 80.2 %copy-start.2 = (s32[32]{0:T(128)S(1)}, s32[32]{0:T(128)}, u32[]{:S(2)}) copy-start(s32[32]{0:T(128)} %param.12) | copy-start | bytes 388
  269.8 160.0 %copy-start = (f32[32]{0:T(128)S(1)}, f32[32]{0:T(128)}, u32[]{:S(2)}) copy-start(f32[32]{0:T(128)} %param.13) | copy-start | bytes 388
  431.7 10.7 %all-to-all-start.1 = ((bf16[8,8,1024]{2,0,1:T(8,128)(2,1)}), bf16[8,8,1024]{2,0,1:T(8,128)(2,1)S(1)}, u32[]{:S(2)}, u32[]{:S(2)}) async-start(bf16[8,8,1024]{2,0,1:T(8,128)(2,1)} %copy.19), calls=%async_computation.2 | async-start | bytes 262144 | tf_op jit(solution)/shard_map/all_to_all | solution.py:81
Sparse Core Ops, SparseCore 0:
  63.7 20.1 all-gather.1
  289.2 140.5 reduce-scatter.1
where the time goes:
time: 453 us; the launch traced here: 450 us
  waiting for transfers between devices  153 us (34%)
  blocking collectives  122 us (27%)
  local copies, waits for them, and re-layouts  87.6 us (19%)
  matrix products  45.4 us (10%)
  between operations  17.6 us (4%)
  other arithmetic  13.3 us (3%)
  starting transfers between devices  10.7 us (2%)
    reduce_scatter x1, waiting for transfers between devices, per_device(): lax.psum_scatter(product, ('dp', 'vocab'), scatter_dimension=0, tiled=True)  141 us
    reshape x1, local copies, waits for them, and re-layouts, per_device(): output_head_matrix.reshape(voc_count, feat_cols, voc_cols)  78.7 us
    psum x1, blocking collectives, per_device(): lax.psum((jnp.sum(shifted, axis=1), picked_local), ('dp', 'vocab'))  41.8 us
    pmax x1, blocking collectives, per_device(): top = lax.pmax(jnp.max(scores, axis=1), ('dp', 'vocab'))  38.6 us
    all_gather x1, blocking collectives, per_device(): gathered_hidden_rows = lax.all_gather(packed, 'dp', axis=0, tiled=True)  33.5 us
    dot_general x1, matrix products, per_device(): jnp.dot(lax.all_gather(gathered_hidden_rows, 'vocab', axis=1, tiled=True)...  21 us
    dot_general x1, matrix products, per_device(): jnp.einsum('ubw,axw->uabx', local_hidden_rows, head_weight_tiles, preferr...  19.2 us
  transfers between devices with their start and end apart: 4, of which 3 were waited for; matrix products, arithmetic and copies ran while one was open for 19% of the time, Pallas kernels for 0%

commit v1 on v0

v1 whole, which is shorter than its diff:
```python
import functools

import jax
import jax.numpy as jnp
from jax import lax
from jax.experimental import pallas as pl
from jax.experimental.pallas import tpu as pltpu
from jax.sharding import PartitionSpec as P

freq_weight = 0.4
presence_weight = 0.8
HALVES = 2
BLOCK = 512
MESH = pl.DeviceIdType.MESH


class Grid:
    def __init__(self, dp_count, voc_count):
        z = 4 if dp_count % 4 == 0 else dp_count
        self.size = {"z": z, "x": dp_count // z, "y": voc_count // 2, "c": 2}

    def me(self):
        dp, voc = lax.axis_index("dp"), lax.axis_index("vocab")
        x, c = self.size["x"], self.size["c"]
        return {
            "z": lax.div(dp, x),
            "x": lax.rem(dp, x),
            "y": lax.div(voc, c),
            "c": lax.rem(voc, c),
        }

    def other(self, me, axis, step):
        return lax.rem(me[axis] + step, self.size[axis])

    def device(self, me, axis, at):
        there = dict(me)
        there[axis] = at
        return (
            there["z"] * self.size["x"] + there["x"],
            there["y"] * self.size["c"] + there["c"],
        )

    def barrier(self, me):
        barrier = pltpu.get_barrier_semaphore()
        peers = 0
        for axis in "zxyc":
            for step in range(1, self.size[axis]):
                pl.semaphore_signal(
                    barrier,
                    inc=1,
                    device_id=self.device(me, axis, self.other(me, axis, step)),
                    device_id_type=MESH,
                )
                peers += 1
        pl.semaphore_wait(barrier, peers)


GATHER_ORDERS = ("zxy", "zyx")
SCATTER_ORDERS = ("yxz", "xyz")


def gather_kernel(grid, x_ref, out_ref, send_sem, recv_sem):
    me = grid.me()
    tok_rows, cols = x_ref.shape
    width = cols // HALVES
    for h in range(HALVES):
        out_ref[me["c"], h, me["y"], me["z"], me["x"]] = x_ref[:, h * width : (h + 1) * width]
    grid.barrier(me)
    used = [0]

    def region(h, have, c=None):
        at = [
            pl.ds(0, grid.size[a]) if a in have else pl.ds(have_at(a, h), 1) for a in "yzx"
        ]
        return out_ref.at[me["c"], h, at[0], at[1], at[2]]

    def have_at(a, h):
        return me[a]

    def start(ref, axis, step):
        k = used[0]
        used[0] += 1
        copy = pltpu.make_async_remote_copy(
            src_ref=ref,
            dst_ref=ref,
            send_sem=send_sem.at[k],
            recv_sem=recv_sem.at[k],
            device_id=grid.device(me, axis, grid.other(me, axis, step)),
            device_id_type=MESH,
        )
        copy.start()
        return copy

    core_copies = []
    stages = len(GATHER_ORDERS[0])
    for s in range(stages):
        copies = []
        for h in range(HALVES):
            order = GATHER_ORDERS[h]
            ref = region(h, order[:s])
            for step in range(1, grid.size[order[s]]):
                copies.append(start(ref, order[s], step))
        if s == stages - 1:
            for h in range(HALVES):
                core_copies.append(start(region(h, GATHER_ORDERS[h][:s]), "c", 1))
        for copy in copies:
            copy.wait()
    for h in range(HALVES):
        order = GATHER_ORDERS[h]
        last = order[-1]
        for step in range(1, grid.size[last]):
            at = [
                pl.ds(grid.other(me, a, step), 1) if a == last else pl.ds(0, grid.size[a])
                for a in "yzx"
            ]
            core_copies.append(start(out_ref.at[me["c"], h, at[0], at[1], at[2]], "c", 1))
    for copy in core_copies:
        copy.wait()


def gather_rows(grid, packed):
    tok_rows, cols = packed.shape
    size = grid.size
    n = HALVES * (size["z"] + size["x"] + size["y"] + size["x"] + size["y"])
    shape = (2, HALVES, size["y"], size["z"], size["x"], tok_rows, cols // HALVES)
    out = pl.pallas_call(
        functools.partial(gather_kernel, grid),
        name="gather_rows",
        out_shape=jax.ShapeDtypeStruct(shape, packed.dtype),
        in_specs=[pl.BlockSpec(memory_space=pltpu.VMEM)],
        out_specs=pl.BlockSpec(memory_space=pltpu.VMEM),
        scratch_shapes=[pltpu.SemaphoreType.DMA((n,)), pltpu.SemaphoreType.DMA((n,))],
        compiler_params=pltpu.CompilerParams(
            collective_id=0, has_side_effects=True, vmem_limit_bytes=24 << 20
        ),
    )(packed)
    return out.reshape(shape[:3] + (size["z"] * size["x"] * tok_rows, cols // HALVES))


def stats_kernel(grid, stats_ref, logprob_ref, top_ref, *scratch):
    me = grid.me()
    slots, (send_sem, recv_sem) = dict(zip("yxzc", scratch[:4])), scratch[4:]
    lanes = stats_ref.shape[1]
    held = jnp.transpose(stats_ref[...])[:8]
    top, total, picked = held[0:1], held[1:2], held[2:3]
    grid.barrier(me)
    used = 0
    for axis in "yxzc":
        n = grid.size[axis]
        if n == 1:
            continue
        slot = slots[axis]
        slot[me[axis]] = jnp.concatenate([top, total, picked, jnp.zeros_like(held[3:])], axis=0)
        copies = []
        for step in range(1, n):
            copy = pltpu.make_async_remote_copy(
                src_ref=slot.at[me[axis]],
                dst_ref=slot.at[me[axis]],
                send_sem=send_sem.at[used],
                recv_sem=recv_sem.at[used],
                device_id=grid.device(me, axis, grid.other(me, axis, step)),
                device_id_type=MESH,
            )
            copy.start()
            copies.append(copy)
            used += 1
        for copy in copies:
            copy.wait()
        blocks = [slot[k] for k in range(n)]
        top = functools.reduce(jnp.maximum, [b[0:1] for b in blocks])
        total = sum(b[1:2] * jnp.exp(b[0:1] - top) for b in blocks)
        picked = sum(b[2:3] for b in blocks)
    logprob_ref[...] = jnp.broadcast_to(picked - top - jnp.log(total), logprob_ref.shape)
    rows = top.shape[1]
    both = jnp.concatenate(
        [top, 1.0 / total, jnp.zeros((lanes - 2, rows), jnp.float32)], axis=0
    )
    top_ref[...] = jnp.transpose(both)


def combine_stats(grid, stats):
    rows, lanes = stats.shape
    size = grid.size
    n = sum(size[a] for a in "yxzc")
    vmem = pl.BlockSpec(memory_space=pltpu.VMEM)
    return pl.pallas_call(
        functools.partial(stats_kernel, grid),
        name="combine_stats",
        out_shape=[
            jax.ShapeDtypeStruct((8, rows), jnp.float32),
            jax.ShapeDtypeStruct((rows, lanes), jnp.float32),
        ],
        in_specs=[vmem],
        out_specs=[vmem, vmem],
        scratch_shapes=[pltpu.VMEM((size[a], 8, rows), jnp.float32) for a in "yxzc"]
        + [pltpu.SemaphoreType.DMA((n,)), pltpu.SemaphoreType.DMA((n,))],
        compiler_params=pltpu.CompilerParams(collective_id=1, has_side_effects=True),
    )(stats)


def scatter_kernel(grid, p_ref, out_ref, core_recv, acc, sendbuf, *rest):
    me = grid.me()
    recvs = rest[: HALVES * 3]
    send_sem, recv_sem = rest[HALVES * 3 :]
    used = [0]
    grid.barrier(me)

    def start(src, dst, axis, step):
        k = used[0]
        used[0] += 1
        copy = pltpu.make_async_remote_copy(
            src_ref=src,
            dst_ref=dst,
            send_sem=send_sem.at[k],
            recv_sem=recv_sem.at[k],
            device_id=grid.device(me, axis, grid.other(me, axis, step)),
            device_id_type=MESH,
        )
        copy.start()
        return copy

    there = grid.other(me, "c", 1)
    core = [start(p_ref.at[there, h], core_recv.at[h], "c", 1) for h in range(HALVES)]
    for h in range(HALVES):
        core[h].wait()
        acc[h] = p_ref[me["c"], h] + core_recv[h]

    def cut(h, done, axis, at):
        where = []
        for a in "yzx":
            if a == axis:
                where.append(pl.ds(at, 1))
            elif a in done:
                where.append(pl.ds(me[a], 1))
            else:
                where.append(pl.ds(0, grid.size[a]))
        return (h, where[0], where[1], where[2])

    for s in range(3):
        copies = []
        for h in range(HALVES):
            order = SCATTER_ORDERS[h]
            axis, done = order[s], order[:s]
            recv = recvs[h * 3 + s]
            for step in range(1, grid.size[axis]):
                idx = cut(h, done, axis, grid.other(me, axis, step))
                sendbuf[idx] = acc[idx].astype(sendbuf.dtype)
                copies.append((h, step, start(sendbuf.at[idx], recv.at[step - 1], axis, step)))
        for h, step, copy in copies:
            copy.wait()
            order = SCATTER_ORDERS[h]
            axis, done = order[s], order[:s]
            idx = cut(h, done, axis, me[axis])
            acc[idx] = acc[idx] + recvs[h * 3 + s][step - 1].astype(jnp.float32)
    width = out_ref.shape[1] // HALVES
    for h in range(HALVES):
        out_ref[:, h * width : (h + 1) * width] = acc[h, me["y"], me["z"], me["x"]]


def scatter_sum(grid, product, tok_rows):
    size = grid.size
    width = product.shape[-1]
    part = (HALVES, size["y"], size["z"], size["x"], tok_rows, width)
    product = product.reshape((2,) + part)
    recvs = []
    for h in range(HALVES):
        shape = {a: size[a] for a in "yzx"}
        for axis in SCATTER_ORDERS[h]:
            shape[axis] = 1
            recvs.append(
                pltpu.VMEM(
                    (max(size[axis] - 1, 1),)
                    + tuple(shape[a] for a in "yzx")
                    + (tok_rows, width),
                    jnp.bfloat16,
                )
            )
    n = HALVES * (1 + sum(size[a] for a in "yzx"))
    return pl.pallas_call(
        functools.partial(scatter_kernel, grid),
        name="scatter_sum",
        out_shape=jax.ShapeDtypeStruct((tok_rows, width * HALVES), jnp.float32),
        in_specs=[pl.BlockSpec(memory_space=pltpu.VMEM)],
        out_specs=pl.BlockSpec(memory_space=pltpu.VMEM),
        scratch_shapes=[
            pltpu.VMEM(part, jnp.float32),
            pltpu.VMEM(part, jnp.float32),
            pltpu.VMEM(part, jnp.bfloat16),
        ]
        + recvs
        + [pltpu.SemaphoreType.DMA((n,)), pltpu.SemaphoreType.DMA((n,))],
        compiler_params=pltpu.CompilerParams(
            collective_id=2, has_side_effects=True, vmem_limit_bytes=48 << 20
        ),
    )(product)


def head_rows(grid, c, h, y, width):
    start = (y * grid.size["c"] + c) * HALVES * width + h * width
    return slice(start, start + width)


def pieces(grid):
    return [(c, h, y) for c in range(2) for h in range(HALVES) for y in range(grid.size["y"])]


def forward_kernel(grid, voc_cols, start_ref, x_ref, w_ref, ids_ref, prior_ref, scores_ref, stats_ref):
    j = pl.program_id(0)
    width = x_ref.shape[-1]
    rows = x_ref.shape[-2]
    logits = jnp.zeros((rows, BLOCK), jnp.float32)
    for c, h, y in pieces(grid):
        logits += jnp.dot(
            x_ref[c, h, y],
            w_ref[head_rows(grid, c, h, y, width), :],
            preferred_element_type=jnp.float32,
        )
    column = j * BLOCK + lax.broadcasted_iota(jnp.int32, (rows, BLOCK), 1)
    valid = column < voc_cols
    hits = (ids_ref[...] == column + start_ref[0]) & valid
    counts = jnp.dot(
        prior_ref[...],
        jnp.where(hits, 1.0, 0.0).astype(jnp.bfloat16),
        preferred_element_type=jnp.float32,
    )
    scores = logits - freq_weight * counts - jnp.where(counts > 0, presence_weight, 0.0)
    scores_ref[...] = scores
    picked = jnp.sum(jnp.where(hits, scores, 0.0), axis=1, keepdims=True)
    scores = jnp.where(valid, scores, -jnp.inf)
    lane = lax.broadcasted_iota(jnp.int32, stats_ref.shape, 1)

    @pl.when(j == 0)
    def _():
        stats_ref[...] = jnp.where(lane == 0, -jnp.inf, 0.0)

    old = stats_ref[...]
    top = jnp.maximum(old[:, 0:1], jnp.max(scores, axis=1, keepdims=True))
    total = old[:, 1:2] * jnp.exp(old[:, 0:1] - top) + jnp.sum(
        jnp.exp(scores - top), axis=1, keepdims=True
    )
    stats_ref[...] = jnp.where(
        lane == 0,
        top,
        jnp.where(lane == 1, total, jnp.where(lane == 2, old[:, 2:3] + picked, 0.0)),
    )


def forward(grid, x, head, col_start, ids, prior):
    depth, voc_cols = head.shape
    rows = x.shape[-2]
    blocks = pl.cdiv(voc_cols, BLOCK)
    return pl.pallas_call(
        functools.partial(forward_kernel, grid, voc_cols),
        name="forward_scores",
        grid=(blocks,),
        out_shape=[
            jax.ShapeDtypeStruct((rows, voc_cols), jnp.float32),
            jax.ShapeDtypeStruct((rows, 128), jnp.float32),
        ],
        in_specs=[
            pl.BlockSpec(memory_space=pltpu.SMEM),
            pl.BlockSpec(x.shape, lambda j: (0,) * 5),
            pl.BlockSpec((depth, BLOCK), lambda j: (0, j)),
            pl.BlockSpec((rows, 1), lambda j: (0, 0)),
            pl.BlockSpec((rows, rows), lambda j: (0, 0)),
        ],
        out_specs=[
            pl.BlockSpec((rows, BLOCK), lambda j: (0, j)),
            pl.BlockSpec((rows, 128), lambda j: (0, 0)),
        ],
        compiler_params=pltpu.CompilerParams(vmem_limit_bytes=48 << 20),
        cost_estimate=pl.CostEstimate(
            flops=2 * rows * depth * voc_cols,
            bytes_accessed=2 * depth * voc_cols,
            transcendentals=rows * voc_cols,
        ),
    )(col_start, x, head, ids, prior)


def backward_kernel(grid, voc_cols, start_ref, scores_ref, w_ref, ids_ref, top_ref, out_ref):
    j = pl.program_id(0)
    width = out_ref.shape[-1]
    rows = scores_ref.shape[0]
    column = j * BLOCK + lax.broadcasted_iota(jnp.int32, (rows, BLOCK), 1)
    valid = column < voc_cols
    hits = jnp.where(ids_ref[...] == column + start_ref[0], 1.0, 0.0)
    probs = jnp.exp(scores_ref[...] - top_ref[:, 0:1]) * top_ref[:, 1:2]
    residual = jnp.where(valid, hits - probs, 0.0).astype(jnp.bfloat16)
    last = pl.num_programs(0) - 1
    spare = voc_cols % BLOCK != 0

    def add(masked):
        for c, h, y in pieces(grid):
            w = w_ref[head_rows(grid, c, h, y, width), :]
            if masked:
                inside = lax.broadcasted_iota(jnp.int32, w.shape, 1) < voc_cols % BLOCK
                w = jnp.where(inside, w, jnp.zeros_like(w))
            term = lax.dot_general(
                residual, w, (((1,), (1,)), ((), ())), preferred_element_type=jnp.float32
            )
            out_ref[c, h, y] += term

    @pl.when(j == 0)
    def _():
        out_ref[...] = jnp.zeros_like(out_ref)

    if spare:
        pl.when(j != last)(lambda: add(False))
        pl.when(j == last)(lambda: add(True))
    else:
        add(False)


def backward(grid, scores, head, col_start, ids, tops, shape):
    depth, voc_cols = head.shape
    rows = scores.shape[0]
    return pl.pallas_call(
        functools.partial(backward_kernel, grid, voc_cols),
        name="backward_product",
        grid=(pl.cdiv(voc_cols, BLOCK),),
        out_shape=jax.ShapeDtypeStruct(shape, jnp.float32),
        in_specs=[
            pl.BlockSpec(memory_space=pltpu.SMEM),
            pl.BlockSpec((rows, BLOCK), lambda j: (0, j)),
            pl.BlockSpec((depth, BLOCK), lambda j: (0, j)),
            pl.BlockSpec((rows, 1), lambda j: (0, 0)),
            pl.BlockSpec(tops.shape, lambda j: (0, 0)),
        ],
        out_specs=pl.BlockSpec(shape, lambda j: (0,) * 5),
        compiler_params=pltpu.CompilerParams(vmem_limit_bytes=48 << 20),
        cost_estimate=pl.CostEstimate(
            flops=2 * rows * depth * voc_cols,
            bytes_accessed=2 * depth * voc_cols,
            transcendentals=rows * voc_cols,
        ),
    )(col_start, scores, head, ids, tops)


def per_device(hidden, output_head_matrix, row_counts, token_ids, segment_ids, cotangent):
    dp_count = lax.axis_size("dp")
    voc_count = lax.axis_size("vocab")
    dp_index = lax.axis_index("dp")
    grid = Grid(dp_count, voc_count)
    slot_rows, feat_cols = hidden.shape
    per_peer = slot_rows // dp_count
    tok_rows = token_ids.shape[0]
    total_rows = tok_rows * dp_count
    voc_cols = output_head_matrix.shape[1]
    ends = jnp.cumsum(row_counts)
    starts = ends - row_counts
    my_start = starts[dp_index]
    live = jnp.arange(slot_rows, dtype=jnp.int32) < row_counts[dp_index]
    outgoing = jnp.where(live[:, None], hidden, jnp.zeros_like(hidden))
    outgoing = jnp.roll(outgoing.reshape(per_peer, dp_count, feat_cols), my_start, axis=1)
    arrived = lax.all_to_all(outgoing, "dp", split_axis=1, concat_axis=1, tiled=True)
    offsets = jnp.mod(dp_index - starts, dp_count)
    base_pos = (starts + offsets - dp_index) // dp_count
    turns = jnp.arange(per_peer, dtype=jnp.int32)[:, None]
    valid = turns * dp_count + offsets[None, :] < row_counts[None, :]
    target_position = (base_pos[None, :] + turns).reshape(-1)
    placing = (
        target_position[None, :] == jnp.arange(tok_rows, dtype=jnp.int32)[:, None]
    ) & valid.reshape(-1)[None, :]
    placing = placing.astype(jnp.bfloat16)
    packed = jnp.dot(
        placing, arrived.reshape(per_peer * dp_count, feat_cols), preferred_element_type=jnp.float32
    ).astype(jnp.bfloat16)
    both = lax.all_to_all(
        jnp.broadcast_to(jnp.stack([token_ids, segment_ids])[None], (dp_count, 2, tok_rows)),
        "dp",
        split_axis=0,
        concat_axis=0,
        tiled=True,
    )
    ids_all, segs_all = both[:, 0].reshape(-1), both[:, 1].reshape(-1)
    positions = jnp.arange(total_rows, dtype=jnp.int32)
    prior = (
        (segs_all[:, None] == segs_all[None, :]) & (positions[None, :] < positions[:, None])
    ).astype(jnp.bfloat16)
    x = gather_rows(grid, packed)
    col_start = ((dp_index * voc_count + lax.axis_index("vocab")) * voc_cols).reshape(1)
    ids = ids_all[:, None]
    scores, stats = forward(grid, x, output_head_matrix, col_start, ids, prior)
    all_logprobs, tops = combine_stats(grid, stats)
    logprobs = lax.dynamic_slice_in_dim(all_logprobs[0], dp_index * tok_rows, tok_rows, 0)
    product = backward(grid, scores, output_head_matrix, col_start, ids, tops, x.shape)
    summed = scatter_sum(grid, product, tok_rows)
    scaled = (summed * cotangent[:, None]).astype(jnp.bfloat16)
    sending = jnp.dot(placing.T, scaled, preferred_element_type=jnp.float32).astype(jnp.bfloat16)
    sending = sending.reshape(per_peer, dp_count, feat_cols)
    returned = lax.all_to_all(sending, "dp", split_axis=1, concat_axis=1, tiled=True)
    grad_hidden = jnp.roll(returned, -my_start, axis=1).reshape(slot_rows, feat_cols)
    return (logprobs, grad_hidden)


def solution(mesh):
    return jax.shard_map(
        per_device,
        mesh=mesh,
        in_specs=(P("dp", "vocab"), P(None, ("dp", "vocab")), P(), P("dp"), P("dp"), P("dp")),
        out_specs=(P("dp"), P("dp", "vocab")),
        check_vma=False,
    )
```

time: 453 us -> 200 us (0.44)
  waiting for transfers between devices: 153 us -> 12.4 us
  blocking collectives: 122 us -> 0 us
  Pallas kernels: 0 us -> 105 us
  matrix products: 45.4 us -> 0.44 us
  local copies, waits for them, and re-layouts: 87.6 us -> 53.9 us
  between operations: 17.6 us -> 3.49 us
  other arithmetic: 13.3 us -> 5.55 us
  starting transfers between devices: 10.7 us -> 17.3 us
    reduce_scatter x1 -> x0, waiting for transfers between devices: 141 us -> none  [per_device(): lax.psum_scatter(product, ('dp', 'vocab'), scatter_dimension=0, tiled=True)]
    pallas_call x0 -> x5, Pallas kernels: none -> 105 us  [the longest x1 26 us: scatter_sum(): pl.pallas_call(functools.partial(scatter_kernel, grid), name='scatter_sum...]
    reshape x1 -> x0, local copies, waits for them, and re-layouts: 78.7 us -> none  [per_device(): output_head_matrix.reshape(voc_count, feat_cols, voc_cols)]
    unnamed x13 -> x7, local copies, waits for them, and re-layouts: 1.08 us -> 48.2 us
    dot_general x3 -> x0, matrix products: 44 us -> none  [the longest x1 21 us: per_device(): jnp.dot(lax.all_gather(gathered_hidden_rows, 'vocab', axis=1, tiled=True)...]
    psum x1 -> x0, blocking collectives: 41.8 us -> none  [per_device(): lax.psum((jnp.sum(shifted, axis=1), picked_local), ('dp', 'vocab'))]
    pmax x1 -> x0, blocking collectives: 38.6 us -> none  [per_device(): top = lax.pmax(jnp.max(scores, axis=1), ('dp', 'vocab'))]
    all_gather x1 -> x0, blocking collectives: 33.5 us -> none  [per_device(): gathered_hidden_rows = lax.all_gather(packed, 'dp', axis=0, tiled=True)]
  transfers between devices with their start and end apart: 4 -> 3, of which waited for: 3 -> 2; matrix products, arithmetic and copies ran while one was open for 19% -> 28% of each run, Pallas kernels for 0% -> 0%
where the time goes in v1:
time: 200 us; the launch traced here: 198 us
  Pallas kernels  105 us (52%)
  local copies, waits for them, and re-layouts  53.9 us (27%)
  starting transfers between devices  17.3 us (9%)
  waiting for transfers between devices  12.4 us (6%)
  other arithmetic  5.55 us (3%)
  between operations  3.49 us (2%)
    unnamed x7, local copies, waits for them, and re-layouts  48.2 us
    pallas_call x1, Pallas kernels, scatter_sum(): pl.pallas_call(functools.partial(scatter_kernel, grid), name='scatter_sum...  26 us
    pallas_call x1, Pallas kernels, forward(): pl.pallas_call(functools.partial(forward_kernel, grid, voc_cols), name='f...  24.5 us
    pallas_call x1, Pallas kernels, backward(): pl.pallas_call(functools.partial(backward_kernel, grid, voc_cols), name='...  21.3 us
    pallas_call x1, Pallas kernels, gather_rows(): pl.pallas_call(functools.partial(gather_kernel, grid), name='gather_rows'...  18.9 us
    pallas_call x1, Pallas kernels, combine_stats(): pl.pallas_call(functools.partial(stats_kernel, grid), name='combine_stats...  13.9 us
    all_to_all x1, starting transfers between devices, per_device(): lax.all_to_all(jnp.broadcast_to(jnp.stack([token_ids, segment_ids])[None]...  7.25 us
    all_to_all x1, waiting for transfers between devices, per_device(): lax.all_to_all(outgoing, 'dp', split_axis=1, concat_axis=1, tiled=True)  6.99 us
  transfers between devices with their start and end apart: 3, of which 2 were waited for; matrix products, arithmetic and copies ran while one was open for 28% of the time, Pallas kernels for 0%

profile of v1, /device:TPU:0, one launch (start us, length us, event | category | flops | bytes accessed | tf_op | source)
XLA Modules:
  0.0 197.8 jit_solution(12672966513655600581)
XLA Ops:
  0.6 0.7 pad_add_fusion
  1.3 0.6 broadcast_in_dim.14
  1.9 7.3 %all-to-all-start.1 = ((s32[8,2,32]{2,1,0:T(2,128)}), s32[8,2,32]{2,1,0:T(2,128)S(1)}, u32[]{:S(2)}, u32[]{:S(2)}) async-start(s32[8,2,32]{2,1,0:T(2,128)} %broadcast_in_dim.14), calls=%async_computation.1 | async-start | bytes 16384 | tf_op jit(solution)/shard_map/all_to_all | solution.py:468
  9.2 0.8 reduce-window.9
  10.0 0.7 and_select_fusion
  10.7 0.7 dynamic_slice.15
  13.4 1.2 dynamic_slice.14
  14.6 0.6 iota_compare_fusion.2
  15.3 1.0 select_bitcast_fusion
  16.3 0.7 add_compare_fusion
  17.0 0.1 fusion.5
  17.1 0.7 copy.19
  17.9 0.1 add.72
  17.9 0.1 lt.63
  18.0 46.6 %copy.21.w_ref = bf16[4096,4748]{1,0:T(8,128)(2,1)} copy(bf16[4096,4748]{0,1:T(8,128)(2,1)} %param.9) | data formatting | bytes 77791232 | tf_op args[1]
  64.7 0.0 all-to-all-done.1
  64.7 6.0 %all-to-all-start = ((bf16[8,8,1024]{2,0,1:T(8,128)(2,1)}), bf16[8,8,1024]{2,0,1:T(8,128)(2,1)S(1)}, u32[]{:S(2)}, u32[]{:S(2)}) async-start(bf16[8,8,1024]{2,0,1:T(8,128)(2,1)} %copy.19), calls=%async_computation | async-start | bytes 262144 | tf_op jit(solution)/shard_map/all_to_all | solution.py:455
  70.7 0.1 broadcast_in_dim_reshape_squeeze.6.ids_ref
  70.8 0.1 eq.35
  70.9 0.1 fusion.2.prior_ref
  71.0 7.0 %all-to-all-done = bf16[8,8,1024]{2,0,1:T(8,128)(2,1)S(1)} async-done(((bf16[8,8,1024]{2,0,1:T(8,128)(2,1)}), bf16[8,8,1024]{2,0,1:T(8,128)(2,1)S(1)}, u32[]{:S(2)}, u32[]{:S(2)}) %all-to-all-start) | async-done | bytes 131104 | tf_op jit(solution)/shard_map/all_to_all | solution.py:455
  78.0 0.2 convolution_convert_fusion.1.x_ref
  78.2 18.9 %gather_rows.1 = bf16[2,2,2,4,2,32,512]{6,5,4,3,2,1,0:T(8,128)(2,1)S(1)} custom-call(bf16[32,1024]{1,0:T(8,128)(2,1)S(1)} %convolution_convert_fusion.1.x_ref), custom_call_target="tpu_custom_call" | custom-call | tf_op jit(solution)/shard_map/gather_rows/pallas_call | solution.py:126
  97.1 24.5 %forward_scores.1 = (f32[256,4748]{1,0:T(8,128)}, f32[256,128]{1,0:T(8,128)S(1)}) custom-call(s32[1]{0:T(128)} %bitcast.start_ref, bf16[2,2,2,256,512]{4,3,2,1,0:T(8,128)(2,1)S(1)} %bitcast.23, bf16[4096,4748]{1,0:T(8,128)(2,1)} %copy.21.w_ref, s32[256,1]{1,0:T(8,128)S(1)} %broadcast_in_dim_reshape_squeeze.6.ids_ref, bf16[256,256]{1,0:T(8,128)(2,1)S(1)} %fusion.2.prior_ref), custom_call_target="tpu_custom_call" | custom-call | flops 9957277696 | bytes 38895616 | tf_op jit(solution)/shard_map/forward_scores/pallas_call | solution.py:352
  121.6 0.0 copy-start.1
  121.6 0.7 copy-done.1
  122.3 13.9 %combine_stats.1 = (f32[8,256]{1,0:T(8,128)}, f32[256,128]{1,0:T(8,128)}) custom-call(f32[256,128]{1,0:T(8,128)} %copy-done.1), custom_call_target="tpu_custom_call" | custom-call | tf_op jit(solution)/shard_map/combine_stats/pallas_call | solution.py:186
  136.2 0.0 copy-start
  136.3 0.9 copy-done
  137.2 0.0 copy-start.2
  137.2 21.3 %backward_product.1 = f32[2,2,2,256,512]{4,3,2,1,0:T(8,128)S(1)} custom-call(s32[1]{0:T(128)} %bitcast.start_ref, f32[256,4748]{1,0:T(8,128)} %get-tuple-element.9.scores_ref, bf16[4096,4748]{1,0:T(8,128)(2,1)} %copy.21.w_ref, s32[256,1]{1,0:T(8,128)S(1)} %broadcast_in_dim_reshape_squeeze.6.ids_ref, f32[256,128]{1,0:T(8,128)S(1)} %copy-done), custom_call_target="tpu_custom_call" | custom-call | flops 9957277696 | bytes 38895616 | tf_op jit(solution)/shard_map/backward_product/pallas_call | solution.py:417
  158.5 26.0 %scatter_sum.1 = f32[32,1024]{1,0:T(8,128)S(1)} custom-call(f32[2,2,2,4,2,32,512]{6,5,4,3,2,1,0:T(8,128)S(1)} %bitcast.22), custom_call_target="tpu_custom_call" | custom-call | tf_op jit(solution)/shard_map/scatter_sum/pallas_call | solution.py:279
  184.5 0.0 copy-done.2
  184.5 0.2 fusion
  184.7 0.7 copy.25
  185.5 4.1 %all-to-all-start.2 = ((bf16[8,8,1024]{2,0,1:T(8,128)(2,1)}), bf16[8,8,1024]{2,0,1:T(8,128)(2,1)S(1)}, u32[]{:S(2)}, u32[]{:S(2)}) async-start(bf16[8,8,1024]{2,0,1:T(8,128)(2,1)} %copy.25), calls=%async_computation.2 | async-start | bytes 262144 | tf_op jit(solution)/shard_map/all_to_all | solution.py:491
  190.3 0.7 slice.11
  191.0 0.6 fusion.16
  191.5 5.4 %all-to-all-done.2 = bf16[8,8,1024]{2,0,1:T(8,128)(2,1)S(1)} async-done(((bf16[8,8,1024]{2,0,1:T(8,128)(2,1)}), bf16[8,8,1024]{2,0,1:T(8,128)(2,1)S(1)}, u32[]{:S(2)}, u32[]{:S(2)}) %all-to-all-start.2) | async-done | bytes 131104 | tf_op jit(solution)/shard_map/all_to_all | solution.py:491
  196.9 0.1 copy.26
  197.0 0.8 fusion.4
  (3 shorter events, 0.0 us)
Async XLA Ops:
  1.9 62.7 %all-to-all-start.1 = ((s32[8,2,32]{2,1,0:T(2,128)}), s32[8,2,32]{2,1,0:T(2,128)S(1)}, u32[]{:S(2)}, u32[]{:S(2)}) async-start(s32[8,2,32]{2,1,0:T(2,128)} %broadcast_in_dim.14), calls=%async_computation.1 | async-start | bytes 16384 | tf_op jit(solution)/shard_map/all_to_all | solution.py:468
  64.7 13.3 %all-to-all-start = ((bf16[8,8,1024]{2,0,1:T(8,128)(2,1)}), bf16[8,8,1024]{2,0,1:T(8,128)(2,1)S(1)}, u32[]{:S(2)}, u32[]{:S(2)}) async-start(bf16[8,8,1024]{2,0,1:T(8,128)(2,1)} %copy.19), calls=%async_computation | async-start | bytes 262144 | tf_op jit(solution)/shard_map/all_to_all | solution.py:455
  121.6 0.7 copy-start.1
  136.2 0.9 copy-start
  137.2 47.3 %copy-start.2 = (f32[32]{0:T(128)S(1)}, f32[32]{0:T(128)}, u32[]{:S(2)}) copy-start(f32[32]{0:T(128)} %param.13) | copy-start | bytes 388
  185.5 11.4 %all-to-all-start.2 = ((bf16[8,8,1024]{2,0,1:T(8,128)(2,1)}), bf16[8,8,1024]{2,0,1:T(8,128)(2,1)S(1)}, u32[]{:S(2)}, u32[]{:S(2)}) async-start(bf16[8,8,1024]{2,0,1:T(8,128)(2,1)} %copy.25), calls=%async_computation.2 | async-start | bytes 262144 | tf_op jit(solution)/shard_map/all_to_all | solution.py:491

commit v2 on v1

v2 whole, which is shorter than its diff:
```python
import functools

import jax
import jax.numpy as jnp
from jax import lax
from jax.experimental import pallas as pl
from jax.experimental.pallas import tpu as pltpu
from jax.sharding import PartitionSpec as P

freq_weight = 0.4
presence_weight = 0.8
HALVES = 2
BLOCK = 512
MESH = pl.DeviceIdType.MESH


class Grid:
    def __init__(self, dp_count, voc_count):
        z = 4 if dp_count % 4 == 0 else dp_count
        self.size = {"z": z, "x": dp_count // z, "y": voc_count // 2, "c": 2}

    def me(self):
        dp, voc = lax.axis_index("dp"), lax.axis_index("vocab")
        x, c = self.size["x"], self.size["c"]
        return {
            "z": lax.div(dp, x),
            "x": lax.rem(dp, x),
            "y": lax.div(voc, c),
            "c": lax.rem(voc, c),
        }

    def other(self, me, axis, step):
        return lax.rem(me[axis] + step, self.size[axis])

    def device(self, me, axis, at):
        there = dict(me)
        there[axis] = at
        return (
            there["z"] * self.size["x"] + there["x"],
            there["y"] * self.size["c"] + there["c"],
        )

    def groups(self, me):
        dp, voc = lax.axis_index("dp"), lax.axis_index("vocab")
        dp_count = self.size["z"] * self.size["x"]
        voc_count = self.size["y"] * self.size["c"]
        along_dp = [(lax.rem(dp + k, dp_count), voc) for k in range(1, dp_count)]
        along_voc = [(dp, lax.rem(voc + k, voc_count)) for k in range(1, voc_count)]
        return along_dp, along_voc

    def barrier(self, me):
        barrier = pltpu.get_barrier_semaphore()
        along_dp, along_voc = self.groups(me)
        for device in along_dp + along_voc:
            pl.semaphore_signal(barrier, inc=1, device_id=device, device_id_type=MESH)
        pl.semaphore_wait(barrier, len(along_dp) + len(along_voc))


class Sender:
    def __init__(self, send_sem, recv_sem):
        self.send_sem, self.recv_sem, self.used = send_sem, recv_sem, 0

    def start(self, src, dst, device):
        k = self.used
        self.used += 1
        copy = pltpu.make_async_remote_copy(
            src_ref=src,
            dst_ref=dst,
            send_sem=self.send_sem.at[k],
            recv_sem=self.recv_sem.at[k],
            device_id=device,
            device_id_type=MESH,
        )
        copy.start()
        return copy


GATHER_ORDERS = ("zxy", "zyx")
SCATTER_ORDERS = ("yxz", "xyz", "yxz", "xyz")
PARTS = len(SCATTER_ORDERS)


def gather_kernel(
    grid, cols, sent_ref, placing_ref, ids_ref, out_ref, ids_out, arrived, send_sem, recv_sem
):
    me = grid.me()
    dp = lax.axis_index("dp")
    width = cols // HALVES
    sender = Sender(send_sem, recv_sem)
    ids_out[me["z"], me["x"]] = ids_ref[...]
    arrived[dp] = sent_ref[dp]
    grid.barrier(me)
    along_dp, _ = grid.groups(me)
    copies = [sender.start(sent_ref.at[d[0]], arrived.at[dp], d) for d in along_dp]
    id_copies = []

    def send_ids(axis, have):
        at = [pl.ds(0, grid.size[a]) if a in have else pl.ds(me[a], 1) for a in "zx"]
        ref = ids_out.at[at[0], at[1]]
        for step in range(1, grid.size[axis]):
            device = grid.device(me, axis, grid.other(me, axis, step))
            id_copies.append(sender.start(ref, ref, device))

    send_ids("z", "")
    for copy in copies:
        copy.wait()
    blocks, group_rows, group_cols = arrived.shape
    flat = arrived[...].reshape(blocks * group_rows, group_cols)
    packed = jnp.concatenate(
        [
            jnp.dot(placing_ref[g], flat, preferred_element_type=jnp.float32)
            for g in range(cols // group_cols)
        ],
        axis=1,
    ).astype(out_ref.dtype)
    for h in range(HALVES):
        out_ref[me["c"], h, me["y"], me["z"], me["x"]] = packed[:, h * width : (h + 1) * width]

    def start(h, where, axis, step):
        at = [where[a] for a in "yzx"]
        ref = out_ref.at[me["c"], h, at[0], at[1], at[2]]
        return sender.start(ref, ref, grid.device(me, axis, grid.other(me, axis, step)))

    def held(have):
        return {a: pl.ds(0, grid.size[a]) if a in have else pl.ds(me[a], 1) for a in "yzx"}

    stages = len(GATHER_ORDERS[0])
    running = [[] for _ in range(HALVES)]
    core_copies = []
    for s in range(stages + 1):
        for h in range(HALVES):
            order = GATHER_ORDERS[h]
            for copy in running[h]:
                copy.wait()
            if s == stages:
                last = order[-1]
                for step in range(1, grid.size[last]):
                    where = held(order)
                    where[last] = pl.ds(grid.other(me, last, step), 1)
                    core_copies.append(start(h, where, "c", 1))
                continue
            axis, where = order[s], held(order[:s])
            running[h] = [start(h, where, axis, step) for step in range(1, grid.size[axis])]
            if s == stages - 1:
                core_copies.append(start(h, where, "c", 1))
        if s == 0:
            for copy in list(id_copies):
                copy.wait()
            id_copies.clear()
            send_ids("x", "z")
    for copy in id_copies + core_copies:
        copy.wait()


def gather_rows(grid, sent, placing, ids, cols):
    blocks = sent.shape[0]
    tok_rows = placing.shape[1]
    size = grid.size
    n = blocks + size["z"] + size["x"]
    n += HALVES * (size["z"] + size["x"] + size["y"] + size["x"] + size["y"])
    shape = (2, HALVES, size["y"], size["z"], size["x"], tok_rows, cols // HALVES)
    vmem = pl.BlockSpec(memory_space=pltpu.VMEM)
    out, ids_all = pl.pallas_call(
        functools.partial(gather_kernel, grid, cols),
        name="gather_rows",
        out_shape=[
            jax.ShapeDtypeStruct(shape, sent.dtype),
            jax.ShapeDtypeStruct((size["z"], size["x"]) + ids.shape, ids.dtype),
        ],
        in_specs=[vmem] * 3,
        out_specs=[vmem] * 2,
        scratch_shapes=[
            pltpu.VMEM(sent.shape, sent.dtype),
            pltpu.SemaphoreType.DMA((n,)),
            pltpu.SemaphoreType.DMA((n,)),
        ],
        compiler_params=pltpu.CompilerParams(
            collective_id=0, has_side_effects=True, vmem_limit_bytes=24 << 20
        ),
    )(sent, placing, ids)
    return out.reshape(shape[:3] + (blocks * tok_rows, cols // HALVES)), ids_all


def stats_kernel(grid, stats_ref, logprob_ref, top_ref, voc_slots, dp_slots, send_sem, recv_sem):
    me = grid.me()
    along_dp, along_voc = grid.groups(me)
    sender = Sender(send_sem, recv_sem)
    held = stats_ref[...]
    spare = jnp.zeros_like(held[3:])
    grid.barrier(me)
    for slots, at, peers in (
        (voc_slots, lax.axis_index("vocab"), along_voc),
        (dp_slots, lax.axis_index("dp"), along_dp),
    ):
        slots[at] = held
        copies = [sender.start(slots.at[at], slots.at[at], device) for device in peers]
        for copy in copies:
            copy.wait()
        blocks = [slots[k] for k in range(slots.shape[0])]
        top = functools.reduce(jnp.maximum, [b[0:1] for b in blocks])
        total = sum(b[1:2] * jnp.exp(b[0:1] - top) for b in blocks)
        picked = sum(b[2:3] for b in blocks)
        held = jnp.concatenate([top, total, picked, spare], axis=0)
    logprob_ref[...] = jnp.broadcast_to(picked - top - jnp.log(total), logprob_ref.shape)
    top_ref[...] = jnp.concatenate([top, 1.0 / total, picked, spare], axis=0)


def combine_stats(grid, stats):
    size = grid.size
    voc_count, dp_count = size["y"] * size["c"], size["z"] * size["x"]
    n = voc_count + dp_count
    vmem = pl.BlockSpec(memory_space=pltpu.VMEM)
    return pl.pallas_call(
        functools.partial(stats_kernel, grid),
        name="combine_stats",
        out_shape=[jax.ShapeDtypeStruct(stats.shape, jnp.float32)] * 2,
        in_specs=[vmem],
        out_specs=[vmem, vmem],
        scratch_shapes=[
            pltpu.VMEM((voc_count,) + stats.shape, jnp.float32),
            pltpu.VMEM((dp_count,) + stats.shape, jnp.float32),
            pltpu.SemaphoreType.DMA((n,)),
            pltpu.SemaphoreType.DMA((n,)),
        ],
        compiler_params=pltpu.CompilerParams(collective_id=1, has_side_effects=True),
    )(stats)


def scatter_kernel(
    grid, p_ref, cot_ref, placing_ref, out_ref, core_recv, acc, sendbuf, outgoing, *rest
):
    me = grid.me()
    dp = lax.axis_index("dp")
    recvs = rest[: PARTS * 3]
    sender = Sender(*rest[PARTS * 3 :])
    grid.barrier(me)
    there = grid.other(me, "c", 1)
    core = [
        sender.start(p_ref.at[there, h], core_recv.at[h], grid.device(me, "c", there))
        for h in range(PARTS)
    ]

    def cut(h, done, axis, at):
        where = []
        for a in "yzx":
            if a == axis:
                where.append(pl.ds(at, 1))
            elif a in done:
                where.append(pl.ds(me[a], 1))
            else:
                where.append(pl.ds(0, grid.size[a]))
        return (h, where[0], where[1], where[2])

    running = [[] for _ in range(PARTS)]
    for s in range(4):
        for h in range(PARTS):
            order = SCATTER_ORDERS[h]
            if s == 0:
                core[h].wait()
                acc[h] = p_ref[me["c"], h] + core_recv[h]
            else:
                idx = cut(h, order[: s - 1], order[s - 1], me[order[s - 1]])
                for k, copy in enumerate(running[h]):
                    copy.wait()
                    acc[idx] = acc[idx] + recvs[h * 3 + s - 1][k].astype(jnp.float32)
            if s == 3:
                continue
            axis, done = order[s], order[:s]
            running[h] = []
            for step in range(1, grid.size[axis]):
                to = grid.other(me, axis, step)
                idx = cut(h, done, axis, to)
                sendbuf[idx] = acc[idx].astype(sendbuf.dtype)
                running[h].append(
                    sender.start(
                        sendbuf.at[idx], recvs[h * 3 + s].at[step - 1], grid.device(me, axis, to)
                    )
                )
    summed = jnp.concatenate([acc[h, me["y"], me["z"], me["x"]] for h in range(PARTS)], axis=1)
    scaled = (summed * cot_ref[...]).astype(jnp.bfloat16)
    group_cols = outgoing.shape[-1]
    slots = sum(
        jnp.dot(
            placing_ref[g],
            scaled[:, g * group_cols : (g + 1) * group_cols],
            preferred_element_type=jnp.float32,
        )
        for g in range(placing_ref.shape[0])
    )
    outgoing[...] = slots.astype(outgoing.dtype).reshape(outgoing.shape)
    along_dp, _ = grid.groups(me)
    copies = [sender.start(outgoing.at[d[0]], out_ref.at[dp], d) for d in along_dp]
    out_ref[dp] = outgoing[dp]
    for copy in copies:
        copy.wait()


def scatter_sum(grid, product, cotangent, placing, slot_shape):
    size = grid.size
    width = product.shape[-1]
    tok_rows = cotangent.shape[0]
    part = (PARTS, size["y"], size["z"], size["x"], tok_rows, width)
    product = product.reshape((2,) + part)
    recvs = []
    for h in range(PARTS):
        shape = {a: size[a] for a in "yzx"}
        for axis in SCATTER_ORDERS[h]:
            shape[axis] = 1
            recvs.append(
                pltpu.VMEM(
                    (max(size[axis] - 1, 1),)
                    + tuple(shape[a] for a in "yzx")
                    + (tok_rows, width),
                    jnp.bfloat16,
                )
            )
    n = PARTS * (1 + sum(size[a] for a in "yzx")) + slot_shape[0]
    vmem = pl.BlockSpec(memory_space=pltpu.VMEM)
    return pl.pallas_call(
        functools.partial(scatter_kernel, grid),
        name="scatter_sum",
        out_shape=jax.ShapeDtypeStruct(slot_shape, jnp.bfloat16),
        in_specs=[vmem] * 3,
        out_specs=vmem,
        scratch_shapes=[
            pltpu.VMEM(part, jnp.float32),
            pltpu.VMEM(part, jnp.float32),
            pltpu.VMEM(part, jnp.bfloat16),
            pltpu.VMEM(slot_shape, jnp.bfloat16),
        ]
        + recvs
        + [pltpu.SemaphoreType.DMA((n,)), pltpu.SemaphoreType.DMA((n,))],
        compiler_params=pltpu.CompilerParams(
            collective_id=2, has_side_effects=True, vmem_limit_bytes=48 << 20
        ),
    )(product, cotangent[:, None], placing)


def feature_span(grid, parts, c, h, y, width):
    start = (y * grid.size["c"] + c) * parts * width + h * width
    return slice(start, start + width)


def pieces(grid, parts):
    return [(c, h, y) for c in range(2) for h in range(parts) for y in range(grid.size["y"])]


def forward_kernel(
    grid, voc_cols, start_ref, x_ref, w_ref, ids_ref, prior_ref, scores_ref, stats_ref, xt_ref
):
    j = pl.program_id(0)
    width = x_ref.shape[-1]
    rows = x_ref.shape[-2]
    row = lax.broadcasted_iota(jnp.int32, stats_ref.shape, 0)

    @pl.when(j == 0)
    def _():
        stats_ref[...] = jnp.where(row == 0, -jnp.inf, 0.0)
        for c, h, y in pieces(grid, HALVES):
            span = feature_span(grid, HALVES, c, h, y, width)
            xt_ref[span, :] = jnp.transpose(x_ref[c, h, y])

    logits = jnp.dot(w_ref[...], xt_ref[...], preferred_element_type=jnp.float32)
    column = j * BLOCK + lax.broadcasted_iota(jnp.int32, (BLOCK, rows), 0)
    valid = column < voc_cols
    hits = (ids_ref[...] == column + start_ref[0]) & valid
    counts = jnp.dot(
        jnp.where(hits, 1.0, 0.0).astype(jnp.bfloat16),
        prior_ref[...],
        preferred_element_type=jnp.float32,
    )
    scores = logits - freq_weight * counts - jnp.where(counts > 0, presence_weight, 0.0)
    scores_ref[...] = scores
    picked = jnp.sum(jnp.where(hits, scores, 0.0), axis=0, keepdims=True)
    scores = jnp.where(valid, scores, -jnp.inf)
    old = stats_ref[...]
    top = jnp.maximum(old[0:1], jnp.max(scores, axis=0, keepdims=True))
    total = old[1:2] * jnp.exp(old[0:1] - top) + jnp.sum(
        jnp.exp(scores - top), axis=0, keepdims=True
    )
    stats_ref[...] = jnp.concatenate([top, total, old[2:3] + picked, old[3:]], axis=0)


def forward(grid, x, head, col_start, ids, prior):
    voc_cols, depth = head.shape
    rows = x.shape[-2]
    return pl.pallas_call(
        functools.partial(forward_kernel, grid, voc_cols),
        name="forward_scores",
        grid=(pl.cdiv(voc_cols, BLOCK),),
        out_shape=[
            jax.ShapeDtypeStruct((voc_cols, rows), jnp.float32),
            jax.ShapeDtypeStruct((8, rows), jnp.float32),
        ],
        in_specs=[
            pl.BlockSpec(memory_space=pltpu.SMEM),
            pl.BlockSpec(x.shape, lambda j: (0,) * 5),
            pl.BlockSpec((BLOCK, depth), lambda j: (j, 0)),
            pl.BlockSpec((1, rows), lambda j: (0, 0)),
            pl.BlockSpec((rows, rows), lambda j: (0, 0)),
        ],
        out_specs=[
            pl.BlockSpec((BLOCK, rows), lambda j: (j, 0)),
            pl.BlockSpec((8, rows), lambda j: (0, 0)),
        ],
        scratch_shapes=[pltpu.VMEM((depth, rows), x.dtype)],
        compiler_params=pltpu.CompilerParams(vmem_limit_bytes=48 << 20),
        cost_estimate=pl.CostEstimate(
            flops=2 * rows * depth * voc_cols,
            bytes_accessed=2 * depth * voc_cols,
            transcendentals=rows * voc_cols,
        ),
    )(col_start, x, head, ids, prior)


def backward_kernel(grid, voc_cols, start_ref, scores_ref, w_ref, ids_ref, top_ref, out_ref):
    j = pl.program_id(0)
    width = out_ref.shape[-1]
    rows = scores_ref.shape[1]
    column = j * BLOCK + lax.broadcasted_iota(jnp.int32, (BLOCK, rows), 0)
    valid = column < voc_cols
    hits = jnp.where(ids_ref[...] == column + start_ref[0], 1.0, 0.0)
    probs = jnp.exp(scores_ref[...] - top_ref[0:1]) * top_ref[1:2]
    residual = jnp.transpose(jnp.where(valid, hits - probs, 0.0)).astype(jnp.bfloat16)
    last = pl.num_programs(0) - 1
    tail = voc_cols % BLOCK

    def add(masked):
        for c, h, y in pieces(grid, PARTS):
            w = w_ref[:, feature_span(grid, PARTS, c, h, y, width)]
            if masked:
                inside = lax.broadcasted_iota(jnp.int32, w.shape, 0) < tail
                w = jnp.where(inside, w, jnp.zeros_like(w))
            out_ref[c, h, y] += jnp.dot(residual, w, preferred_element_type=jnp.float32)

    @pl.when(j == 0)
    def _():
        out_ref[...] = jnp.zeros_like(out_ref)

    if tail:
        pl.when(j != last)(lambda: add(False))
        pl.when(j == last)(lambda: add(True))
    else:
        add(False)


def backward(grid, scores, head, col_start, ids, tops, shape):
    voc_cols, depth = head.shape
    rows = scores.shape[1]
    return pl.pallas_call(
        functools.partial(backward_kernel, grid, voc_cols),
        name="backward_product",
        grid=(pl.cdiv(voc_cols, BLOCK),),
        out_shape=jax.ShapeDtypeStruct(shape, jnp.float32),
        in_specs=[
            pl.BlockSpec(memory_space=pltpu.SMEM),
            pl.BlockSpec((BLOCK, rows), lambda j: (j, 0)),
            pl.BlockSpec((BLOCK, depth), lambda j: (j, 0)),
            pl.BlockSpec((1, rows), lambda j: (0, 0)),
            pl.BlockSpec(tops.shape, lambda j: (0, 0)),
        ],
        out_specs=pl.BlockSpec(shape, lambda j: (0,) * 5),
        compiler_params=pltpu.CompilerParams(vmem_limit_bytes=48 << 20),
        cost_estimate=pl.CostEstimate(
            flops=2 * rows * depth * voc_cols,
            bytes_accessed=2 * depth * voc_cols,
            transcendentals=rows * voc_cols,
        ),
    )(col_start, scores, head, ids, tops)


def per_device(hidden, output_head_matrix, row_counts, token_ids, segment_ids, cotangent):
    dp_count = lax.axis_size("dp")
    voc_count = lax.axis_size("vocab")
    dp_index = lax.axis_index("dp")
    grid = Grid(dp_count, voc_count)
    slot_rows, feat_cols = hidden.shape
    per_peer = slot_rows // dp_count
    tok_rows = token_ids.shape[0]
    total_rows = tok_rows * dp_count
    voc_cols = output_head_matrix.shape[1]
    groups = max(1, 16 // per_peer)
    group_cols = feat_cols // groups
    ends = jnp.cumsum(row_counts)
    starts = ends - row_counts
    my_start = starts[dp_index]
    live = jnp.arange(slot_rows, dtype=jnp.int32) < row_counts[dp_index]
    outgoing = jnp.where(live[:, None], hidden, jnp.zeros_like(hidden))
    outgoing = jnp.roll(outgoing.reshape(per_peer, dp_count, feat_cols), my_start, axis=1)
    outgoing = outgoing.reshape(per_peer, dp_count, groups, group_cols)
    outgoing = outgoing.transpose(1, 2, 0, 3).reshape(dp_count, groups * per_peer, group_cols)
    offsets = jnp.mod(dp_index - starts, dp_count)
    base_pos = (starts + offsets - dp_index) // dp_count
    turns = jnp.arange(per_peer, dtype=jnp.int32)[None, :]
    valid = turns * dp_count + offsets[:, None] < row_counts[:, None]
    target = jnp.where(valid, base_pos[:, None] + turns, -1)
    group = jnp.arange(groups, dtype=jnp.int32)
    target = jnp.where(
        (group[:, None] == group[None, :])[:, None, :, None], target[None, :, None, :], -1
    ).reshape(groups, dp_count * groups * per_peer)
    tok = jnp.arange(tok_rows, dtype=jnp.int32)
    placing = (target[:, None, :] == tok[None, :, None]).astype(jnp.bfloat16)
    placing_back = (target[:, :, None] == tok[None, None, :]).astype(jnp.bfloat16)
    own_ids = jnp.pad(jnp.stack([token_ids, segment_ids]), ((0, 6), (0, 128 - tok_rows)))
    x, ids_all = gather_rows(grid, outgoing, placing, own_ids, feat_cols)
    ids_all = ids_all.reshape(dp_count, 8, 128)[:, :2, :tok_rows]
    ids, segs = ids_all[:, 0].reshape(-1), ids_all[:, 1].reshape(-1)
    positions = jnp.arange(total_rows, dtype=jnp.int32)
    prior = (
        (segs[:, None] == segs[None, :]) & (positions[:, None] < positions[None, :])
    ).astype(jnp.bfloat16)
    col_start = ((dp_index * voc_count + lax.axis_index("vocab")) * voc_cols).reshape(1)
    ids = ids[None, :]
    head = output_head_matrix.T
    scores, stats = forward(grid, x, head, col_start, ids, prior)
    all_logprobs, tops = combine_stats(grid, stats)
    logprobs = lax.dynamic_slice_in_dim(all_logprobs[0], dp_index * tok_rows, tok_rows, 0)
    shape = (2, PARTS, grid.size["y"], total_rows, feat_cols // PARTS)
    product = backward(grid, scores, head, col_start, ids, tops, shape)
    returned = scatter_sum(grid, product, cotangent, placing_back, outgoing.shape)
    returned = returned.reshape(dp_count, groups, per_peer, group_cols)
    returned = returned.transpose(2, 0, 1, 3).reshape(per_peer, dp_count, feat_cols)
    grad_hidden = jnp.roll(returned, -my_start, axis=1).reshape(slot_rows, feat_cols)
    return (logprobs, grad_hidden)


def solution(mesh):
    return jax.shard_map(
        per_device,
        mesh=mesh,
        in_specs=(P("dp", "vocab"), P(None, ("dp", "vocab")), P(), P("dp"), P("dp"), P("dp")),
        out_specs=(P("dp"), P("dp", "vocab")),
        check_vma=False,
    )
```

time: 200 us -> 130 us (0.65)
  local copies, waits for them, and re-layouts: 53.9 us -> 9.44 us
  starting transfers between devices: 17.3 us -> 0 us
  waiting for transfers between devices: 12.4 us -> 0 us
  Pallas kernels: 105 us -> 111 us
    unnamed x7 -> x10, local copies, waits for them, and re-layouts: 48.2 us -> 5.4 us
    all_to_all x3 -> x0, starting transfers between devices: 17.3 us -> none  [the longest x1 7.25 us: per_device(): lax.all_to_all(jnp.broadcast_to(jnp.stack([token_ids, segment_ids])[None]...]
    all_to_all x3 -> x0, waiting for transfers between devices: 12.4 us -> none  [the longest x1 6.99 us: per_device(): lax.all_to_all(outgoing, 'dp', split_axis=1, concat_axis=1, tiled=True)]
    pallas_call x1, Pallas kernels: 18.9 us -> 29.5 us  [gather_rows(): pl.pallas_call(functools.partial(gather_kernel, grid, cols), name='gather...]
    pallas_call x1, Pallas kernels: 13.9 us -> 10.1 us  [combine_stats(): pl.pallas_call(functools.partial(stats_kernel, grid), name='combine_stats...]
    pallas_call x1, Pallas kernels: 24.5 us -> 22.3 us  [forward(): pl.pallas_call(functools.partial(forward_kernel, grid, voc_cols), name='f...]
  transfers between devices with their start and end apart: 3 -> 0, of which waited for: 2 -> 0; matrix products, arithmetic and copies ran while one was open for 28% -> 0% of each run, Pallas kernels for 0% -> 0%
where the time goes in v2:
time: 130 us; the launch traced here: 129 us
  Pallas kernels  111 us (85%)
  local copies, waits for them, and re-layouts  9.44 us (7%)
  other arithmetic  5.68 us (4%)
  between operations  3.32 us (3%)
    pallas_call x1, Pallas kernels, gather_rows(): pl.pallas_call(functools.partial(gather_kernel, grid, cols), name='gather...  29.5 us
    pallas_call x1, Pallas kernels, scatter_sum(): pl.pallas_call(functools.partial(scatter_kernel, grid), name='scatter_sum...  27.4 us
    pallas_call x1, Pallas kernels, forward(): pl.pallas_call(functools.partial(forward_kernel, grid, voc_cols), name='f...  22.3 us
    pallas_call x1, Pallas kernels, backward(): pl.pallas_call(functools.partial(backward_kernel, grid, voc_cols), name='...  21.6 us
    pallas_call x1, Pallas kernels, combine_stats(): pl.pallas_call(functools.partial(stats_kernel, grid), name='combine_stats...  10.1 us
    unnamed x10, local copies, waits for them, and re-layouts  5.4 us

profile of v2, /device:TPU:0, one launch (start us, length us, event | category | flops | bytes accessed | tf_op | source)
XLA Modules:
  0.0 129.4 jit_solution(3061022057614216802)
XLA Ops:
  0.6 0.8 reduce-window.9
  1.5 0.7 and_select_fusion
  2.1 0.6 dynamic_slice.15
  4.7 1.2 dynamic_slice.14
  5.9 0.6 iota_compare_fusion.4
  6.6 1.0 select_bitcast_fusion
  7.6 0.1 fusion.4
  7.7 0.1 reshape.173
  7.8 0.1 copy.18
  7.9 0.1 broadcast_in_dim.59
  8.0 0.1 broadcast_in_dim.60
  8.1 0.7 add_select_fusion
  8.8 0.1 broadcast_in_dim.63
  8.9 0.7 pad_add_fusion
  9.6 29.5 %gather_rows.1 = (bf16[2,2,2,4,2,32,512]{6,5,4,3,2,1,0:T(8,128)(2,1)S(1)}, s32[4,2,8,128]{3,2,1,0:T(8,128)S(1)}) custom-call(bf16[8,16,512]{2,1,0:T(8,128)(2,1)S(1)} %bitcast.34, bf16[2,32,128]{2,1,0:T(8,128)(2,1)S(1)} %fusion.6.placing_ref, s32[8,128]{1,0:T(8,128)S(1)} %pad.4.ids_ref), custom_call_target="tpu_custom_call" | custom-call | tf_op jit(solution)/shard_map/gather_rows/pallas_call | solution.py:163
  39.2 0.1 broadcast_in_dim_reshape_squeeze.2.ids_ref
  39.3 0.1 eq.68
  39.3 0.1 fusion.1.prior_ref
  39.4 22.3 %forward_scores.1 = (f32[4748,256]{1,0:T(8,128)}, f32[8,256]{1,0:T(8,128)S(1)}) custom-call(s32[1]{0:T(128)} %bitcast.start_ref, bf16[2,2,2,256,512]{4,3,2,1,0:T(8,128)(2,1)S(1)} %bitcast.32, bf16[4748,4096]{1,0:T(8,128)(2,1)} %bitcast.36, s32[1,256]{1,0:T(1,128)S(1)} %broadcast_in_dim_reshape_squeeze.2.ids_ref, bf16[256,256]{1,0:T(8,128)(2,1)S(1)} %fusion.1.prior_ref), custom_call_target="tpu_custom_call" | custom-call | flops 9957277696 | bytes 38895616 | tf_op jit(solution)/shard_map/forward_scores/pallas_call | solution.py:387
  61.7 0.0 copy-start.3
  61.7 0.6 copy-done.3
  62.3 10.1 %combine_stats.1 = (f32[8,256]{1,0:T(8,128)}, f32[8,256]{1,0:T(8,128)}) custom-call(f32[8,256]{1,0:T(8,128)} %copy-done.3), custom_call_target="tpu_custom_call" | custom-call | tf_op jit(solution)/shard_map/combine_stats/pallas_call | solution.py:213
  72.4 0.7 slice.14
  73.1 0.6 fusion.7
  74.4 0.0 copy-start.2
  74.4 0.7 copy-done.2
  75.1 0.0 copy-start.4
  75.1 21.6 %backward_product.1 = f32[2,4,2,256,256]{4,3,2,1,0:T(8,128)S(1)} custom-call(s32[1]{0:T(128)} %bitcast.start_ref, f32[4748,256]{1,0:T(8,128)} %get-tuple-element.13.scores_ref, bf16[4748,4096]{1,0:T(8,128)(2,1)} %bitcast.37, s32[1,256]{1,0:T(1,128)S(1)} %broadcast_in_dim_reshape_squeeze.2.ids_ref, f32[8,256]{1,0:T(8,128)S(1)} %copy-done.2), custom_call_target="tpu_custom_call" | custom-call | flops 9957277696 | bytes 38895616 | tf_op jit(solution)/shard_map/backward_product/pallas_call | solution.py:450
  96.7 0.0 copy-start
  96.7 1.9 %copy-done = f32[2,4,2,256,256]{4,3,2,1,0:T(8,128)} copy-done((f32[2,4,2,256,256]{4,3,2,1,0:T(8,128)}, f32[2,4,2,256,256]{4,3,2,1,0:T(8,128)S(1)}, u32[]{:S(2)}) %copy-start) | copy-done | bytes 4194328
  98.6 0.0 copy-done.4
  98.6 0.1 copy.12.cot_ref
  98.7 0.1 fusion.5.placing_ref
  98.8 0.0 copy-start.1
  98.8 2.2 %copy-done.1 = f32[2,4,2,256,256]{4,3,2,1,0:T(8,128)S(1)} copy-done((f32[2,4,2,256,256]{4,3,2,1,0:T(8,128)S(1)}, f32[2,4,2,256,256]{4,3,2,1,0:T(8,128)}, u32[]{:S(2)}) %copy-start.1) | copy-done | bytes 4194328
  101.0 27.4 %scatter_sum.1 = bf16[8,16,512]{2,1,0:T(8,128)(2,1)S(1)} custom-call(f32[2,4,2,4,2,32,256]{6,5,4,3,2,1,0:T(8,128)S(1)} %bitcast.31, f32[32,1]{1,0:T(8,128)S(1)} %copy.12.cot_ref, bf16[2,128,32]{2,1,0:T(8,128)(2,1)S(1)} %fusion.5.placing_ref), custom_call_target="tpu_custom_call" | custom-call | tf_op jit(solution)/shard_map/scatter_sum/pallas_call | solution.py:319
  128.4 0.1 copy.17
  128.6 0.1 reshape.179
  128.6 0.8 fusion.3
  (6 shorter events, 0.1 us)
Async XLA Ops:
  61.7 0.6 copy-start.3
  74.4 0.7 copy-start.2
  75.1 23.6 %copy-start.4 = (f32[32]{0:T(128)S(1)}, f32[32]{0:T(128)}, u32[]{:S(2)}) copy-start(f32[32]{0:T(128)} %param.13) | copy-start | bytes 388
  96.7 1.9 %copy-start = (f32[2,4,2,256,256]{4,3,2,1,0:T(8,128)}, f32[2,4,2,256,256]{4,3,2,1,0:T(8,128)S(1)}, u32[]{:S(2)}) copy-start(f32[2,4,2,256,256]{4,3,2,1,0:T(8,128)S(1)} %backward_product.1) | copy-start | bytes 12582916
  98.8 2.2 %copy-start.1 = (f32[2,4,2,256,256]{4,3,2,1,0:T(8,128)S(1)}, f32[2,4,2,256,256]{4,3,2,1,0:T(8,128)}, u32[]{:S(2)}) copy-start(f32[2,4,2,256,256]{4,3,2,1,0:T(8,128)} %copy-done) | copy-start | bytes 12582916

commit v3 on v2

v3 whole, which is shorter than its diff:
```python
import functools

import jax
import jax.numpy as jnp
from jax import lax
from jax.experimental import pallas as pl
from jax.experimental.pallas import tpu as pltpu
from jax.sharding import PartitionSpec as P

freq_weight = 0.4
presence_weight = 0.8
HALVES = 2
BLOCK = 512
MESH = pl.DeviceIdType.MESH


class Grid:
    def __init__(self, dp_count, voc_count):
        z = 4 if dp_count % 4 == 0 else dp_count
        self.size = {"z": z, "x": dp_count // z, "y": voc_count // 2, "c": 2}

    def me(self):
        dp, voc = lax.axis_index("dp"), lax.axis_index("vocab")
        x, c = self.size["x"], self.size["c"]
        return {
            "z": lax.div(dp, x),
            "x": lax.rem(dp, x),
            "y": lax.div(voc, c),
            "c": lax.rem(voc, c),
        }

    def other(self, me, axis, step):
        return lax.rem(me[axis] + step, self.size[axis])

    def device(self, me, axis, at):
        there = dict(me)
        there[axis] = at
        return (
            there["z"] * self.size["x"] + there["x"],
            there["y"] * self.size["c"] + there["c"],
        )

    def groups(self, me):
        dp, voc = lax.axis_index("dp"), lax.axis_index("vocab")
        dp_count = self.size["z"] * self.size["x"]
        voc_count = self.size["y"] * self.size["c"]
        along_dp = [(lax.rem(dp + k, dp_count), voc) for k in range(1, dp_count)]
        along_voc = [(dp, lax.rem(voc + k, voc_count)) for k in range(1, voc_count)]
        return along_dp, along_voc

    def barrier(self, me):
        barrier = pltpu.get_barrier_semaphore()
        along_dp, along_voc = self.groups(me)
        for device in along_dp + along_voc:
            pl.semaphore_signal(barrier, inc=1, device_id=device, device_id_type=MESH)
        pl.semaphore_wait(barrier, len(along_dp) + len(along_voc))


class Sender:
    def __init__(self, send_sem, recv_sem):
        self.send_sem, self.recv_sem, self.used = send_sem, recv_sem, 0

    def start(self, src, dst, device):
        k = self.used
        self.used += 1
        copy = pltpu.make_async_remote_copy(
            src_ref=src,
            dst_ref=dst,
            send_sem=self.send_sem.at[k],
            recv_sem=self.recv_sem.at[k],
            device_id=device,
            device_id_type=MESH,
        )
        copy.start()
        return copy


GATHER_ORDERS = ("zxy", "zyx")
SCATTER_ORDERS = ("yxz", "xyz", "yxz", "xyz")
PARTS = len(SCATTER_ORDERS)


def gather(grid, me, sender, cols, sent_ref, placing_ref, ids_ref, out_ref, ids_out, arrived):
    dp = lax.axis_index("dp")
    width = cols // HALVES
    ids_out[me["z"], me["x"]] = ids_ref[...]
    arrived[dp] = sent_ref[dp]
    grid.barrier(me)
    along_dp, _ = grid.groups(me)
    copies = [sender.start(sent_ref.at[d[0]], arrived.at[dp], d) for d in along_dp]
    id_copies = []

    def send_ids(axis, have):
        at = [pl.ds(0, grid.size[a]) if a in have else pl.ds(me[a], 1) for a in "zx"]
        ref = ids_out.at[at[0], at[1]]
        for step in range(1, grid.size[axis]):
            device = grid.device(me, axis, grid.other(me, axis, step))
            id_copies.append(sender.start(ref, ref, device))

    send_ids("z", "")
    for copy in copies:
        copy.wait()
    blocks, group_rows, group_cols = arrived.shape
    flat = arrived[...].reshape(blocks * group_rows, group_cols)
    packed = jnp.concatenate(
        [
            jnp.dot(placing_ref[g], flat, preferred_element_type=jnp.float32)
            for g in range(cols // group_cols)
        ],
        axis=1,
    ).astype(out_ref.dtype)
    for h in range(HALVES):
        out_ref[me["c"], h, me["y"], me["z"], me["x"]] = packed[:, h * width : (h + 1) * width]

    def start(h, where, axis, step):
        at = [where[a] for a in "yzx"]
        ref = out_ref.at[me["c"], h, at[0], at[1], at[2]]
        return sender.start(ref, ref, grid.device(me, axis, grid.other(me, axis, step)))

    def held(have):
        return {a: pl.ds(0, grid.size[a]) if a in have else pl.ds(me[a], 1) for a in "yzx"}

    stages = len(GATHER_ORDERS[0])
    running = [[] for _ in range(HALVES)]
    core_copies = []
    for s in range(stages + 1):
        for h in range(HALVES):
            order = GATHER_ORDERS[h]
            for copy in running[h]:
                copy.wait()
            if s == stages:
                last = order[-1]
                for step in range(1, grid.size[last]):
                    where = held(order)
                    where[last] = pl.ds(grid.other(me, last, step), 1)
                    core_copies.append(start(h, where, "c", 1))
                continue
            axis, where = order[s], held(order[:s])
            running[h] = [start(h, where, axis, step) for step in range(1, grid.size[axis])]
            if s == stages - 1:
                core_copies.append(start(h, where, "c", 1))
        if s == 0:
            for copy in list(id_copies):
                copy.wait()
            id_copies.clear()
            send_ids("x", "z")
    for copy in id_copies + core_copies:
        copy.wait()


def exchange_stats(grid, sender, held, voc_slots, dp_slots):
    along_dp, along_voc = grid.groups(None)
    for slots, at, peers in (
        (voc_slots, lax.axis_index("vocab"), along_voc),
        (dp_slots, lax.axis_index("dp"), along_dp),
    ):
        slots[at] = held
        copies = [sender.start(slots.at[at], slots.at[at], device) for device in peers]
        for copy in copies:
            copy.wait()
        blocks = [slots[k] for k in range(slots.shape[0])]
        top = functools.reduce(jnp.maximum, [b[0:1] for b in blocks])
        total = sum(b[1:2] * jnp.exp(b[0:1] - top) for b in blocks)
        picked = sum(b[2:3] for b in blocks)
        held = jnp.concatenate([top, total, picked, jnp.zeros_like(held[3:])], axis=0)
    return top, total, picked


def scatter(
    grid, me, sender, core, cot_ref, placing_ref, out_ref, core_recv, acc, sendbuf, outgoing, recvs
):
    dp = lax.axis_index("dp")

    def cut(h, done, axis, at):
        where = []
        for a in "yzx":
            if a == axis:
                where.append(pl.ds(at, 1))
            elif a in done:
                where.append(pl.ds(me[a], 1))
            else:
                where.append(pl.ds(0, grid.size[a]))
        return (h, where[0], where[1], where[2])

    running = [[] for _ in range(PARTS)]
    for s in range(4):
        for h in range(PARTS):
            order = SCATTER_ORDERS[h]
            if s == 0:
                core(h).wait()
                acc[h] = acc[h] + core_recv[h]
            else:
                idx = cut(h, order[: s - 1], order[s - 1], me[order[s - 1]])
                for k, copy in enumerate(running[h]):
                    copy.wait()
                    acc[idx] = acc[idx] + recvs[h * 3 + s - 1][k].astype(jnp.float32)
            if s == 3:
                continue
            axis, done = order[s], order[:s]
            running[h] = []
            for step in range(1, grid.size[axis]):
                to = grid.other(me, axis, step)
                idx = cut(h, done, axis, to)
                sendbuf[idx] = acc[idx].astype(sendbuf.dtype)
                running[h].append(
                    sender.start(
                        sendbuf.at[idx], recvs[h * 3 + s].at[step - 1], grid.device(me, axis, to)
                    )
                )
    summed = jnp.concatenate([acc[h, me["y"], me["z"], me["x"]] for h in range(PARTS)], axis=1)
    scaled = (summed * cot_ref[...]).astype(jnp.bfloat16)
    group_cols = outgoing.shape[-1]
    slots = sum(
        jnp.dot(
            placing_ref[g],
            scaled[:, g * group_cols : (g + 1) * group_cols],
            preferred_element_type=jnp.float32,
        )
        for g in range(placing_ref.shape[0])
    )
    outgoing[...] = slots.astype(outgoing.dtype).reshape(outgoing.shape)
    along_dp, _ = grid.groups(me)
    copies = [sender.start(outgoing.at[d[0]], out_ref.at[dp], d) for d in along_dp]
    out_ref[dp] = outgoing[dp]
    for copy in copies:
        copy.wait()


def feature_span(grid, parts, c, h, y, width):
    start = (y * grid.size["c"] + c) * parts * width + h * width
    return pl.ds(start if isinstance(start, int) else pl.multiple_of(start, width), width)


def head_kernel(
    grid,
    voc_cols,
    head_ref,
    tail_ref,
    sent_ref,
    placing_ref,
    back_ref,
    cot_ref,
    ids_ref,
    logprob_ref,
    out_ref,
    head,
    x,
    xt,
    scores,
    residual,
    product,
    core_recv,
    acc,
    sendbuf,
    arrived,
    outgoing,
    ids_all,
    voc_slots,
    dp_slots,
    load_sem,
    send_sem,
    recv_sem,
    core_send_sem,
    core_recv_sem,
    *recvs,
):
    me = grid.me()
    sender = Sender(send_sem, recv_sem)
    padded, depth = head.shape
    rows = xt.shape[1]
    main = voc_cols // 128 * 128
    full, rest = padded // BLOCK, padded % BLOCK
    loads = []
    for k, start in enumerate(range(0, main, BLOCK)):
        span = pl.ds(start, min(BLOCK, main - start))
        loads.append(pltpu.make_async_copy(head_ref.at[span], head.at[span], load_sem.at[k]))
    if padded > main:
        span = pl.ds(main, padded - main)
        loads.append(pltpu.make_async_copy(tail_ref, head.at[span], load_sem.at[len(loads)]))
    for load in loads:
        load.start()
    cols = depth // (grid.size["y"] * grid.size["c"])
    gather(grid, me, sender, cols, sent_ref, placing_ref, ids_ref, x, ids_all, arrived)

    width = cols // HALVES
    for c in range(2):
        for h in range(HALVES):
            for y in range(grid.size["y"]):
                piece = x[c, h, y].reshape(rows, width)
                xt[feature_span(grid, HALVES, c, h, y, width), :] = jnp.transpose(piece)
    every = sum(
        ids_all[z, k] for z in range(grid.size["z"]) for k in range(grid.size["x"])
    )
    ids = every[0:1]
    segs = jnp.broadcast_to(every[1:2].astype(jnp.float32), (rows, rows))
    earlier = lax.broadcasted_iota(jnp.int32, (rows, rows), 0) < lax.broadcasted_iota(
        jnp.int32, (rows, rows), 1
    )
    prior = jnp.where((segs == jnp.transpose(segs)) & earlier, 1.0, 0.0).astype(jnp.bfloat16)
    col_start = (
        lax.axis_index("dp") * (grid.size["y"] * grid.size["c"]) + lax.axis_index("vocab")
    ) * voc_cols
    for load in loads:
        load.wait()

    def block(start, size):
        return pl.ds(start if isinstance(start, int) else pl.multiple_of(start, BLOCK), size)

    def hits_of(start, size):
        column = start + lax.broadcasted_iota(jnp.int32, (size, rows), 0)
        valid = column < voc_cols
        return valid, (ids == column + col_start) & valid

    def multiply(start, size):
        at = block(start, size)
        scores[at, :] = jnp.dot(head[at, :], xt[...], preferred_element_type=jnp.float32)

    def penalize(start, size, held):
        at = block(start, size)
        valid, hits = hits_of(start, size)
        counts = jnp.dot(
            jnp.where(hits, 1.0, 0.0).astype(jnp.bfloat16),
            prior,
            preferred_element_type=jnp.float32,
        )
        value = (
            scores[at, :] - freq_weight * counts - jnp.where(counts > 0, presence_weight, 0.0)
        )
        scores[at, :] = value
        picked = jnp.sum(jnp.where(hits, value, 0.0), axis=0, keepdims=True)
        value = jnp.where(valid, value, -jnp.inf)
        top = jnp.maximum(held[0:1], jnp.max(value, axis=0, keepdims=True))
        total = held[1:2] * jnp.exp(held[0:1] - top) + jnp.sum(
            jnp.exp(value - top), axis=0, keepdims=True
        )
        return jnp.concatenate([top, total, held[2:3] + picked, held[3:]], axis=0)

    def forward_step(j, held):
        held = penalize((j - 1) * BLOCK, BLOCK, held)
        multiply(j * BLOCK, BLOCK)
        return held

    row = lax.broadcasted_iota(jnp.int32, (8, rows), 0)
    held = jnp.where(row == 0, -jnp.inf, 0.0)
    multiply(0, BLOCK)
    held = lax.fori_loop(1, full, forward_step, held)
    held = penalize((full - 1) * BLOCK, BLOCK, held)
    if rest:
        multiply(full * BLOCK, rest)
        held = penalize(full * BLOCK, rest, held)

    top, total, picked = exchange_stats(grid, sender, held, voc_slots, dp_slots)
    logprob_ref[...] = jnp.broadcast_to(picked - top - jnp.log(total), logprob_ref.shape)
    scale = 1.0 / total

    def residual_step(start, size):
        at = block(start, size)
        valid, hits = hits_of(start, size)
        probs = jnp.exp(scores[at, :] - top) * scale
        value = jnp.where(valid, jnp.where(hits, 1.0, 0.0) - probs, 0.0).astype(jnp.bfloat16)
        residual[:, at] = jnp.transpose(value)

    def residual_loop(j, carry):
        residual_step(j * BLOCK, BLOCK)
        return carry

    lax.fori_loop(0, full, residual_loop, 0)
    if rest:
        residual_step(full * BLOCK, rest)

    part_width = cols // PARTS
    there = grid.other(me, "c", 1)

    def core_copy(h):
        return pltpu.make_async_remote_copy(
            src_ref=product.at[h],
            dst_ref=core_recv.at[h],
            send_sem=core_send_sem.at[h],
            recv_sem=core_recv_sem.at[h],
            device_id=grid.device(me, "c", there),
            device_id_type=MESH,
        )

    def backward_part(h, c, into):
        for y in range(grid.size["y"]):
            span = feature_span(grid, PARTS, c, h, y, part_width)
            term = jnp.dot(residual[...], head[:, span], preferred_element_type=jnp.float32)
            into[h, y] = term.reshape(into.shape[2:])

    def send_part(h, carry):
        backward_part(h, there, product)
        core_copy(h).start()
        return carry

    def keep_part(h, carry):
        backward_part(h, me["c"], acc)
        return carry

    lax.fori_loop(0, PARTS, send_part, 0)
    lax.fori_loop(0, PARTS, keep_part, 0)
    scatter(
        grid,
        me,
        sender,
        core_copy,
        cot_ref,
        back_ref,
        out_ref,
        core_recv,
        acc,
        sendbuf,
        outgoing,
        recvs,
    )


def head_step(grid, head, sent, placing, placing_back, cotangent, ids, total_rows):
    size = grid.size
    voc_cols, depth = head.shape
    dp_count, voc_count = size["z"] * size["x"], size["y"] * size["c"]
    tok_rows = placing.shape[1]
    cols = depth // voc_count
    main = voc_cols // 128 * 128
    padded = -(-voc_cols // 128) * 128
    tail = jnp.pad(head[main:], ((0, main + 128 - voc_cols), (0, 0)))
    x_shape = (2, HALVES, size["y"], size["z"], size["x"], tok_rows, cols // HALVES)
    part = (PARTS, size["y"], size["z"], size["x"], tok_rows, cols // PARTS)
    recvs = []
    for h in range(PARTS):
        shape = {a: size[a] for a in "yzx"}
        for axis in SCATTER_ORDERS[h]:
            shape[axis] = 1
            recvs.append(
                pltpu.VMEM(
                    (max(size[axis] - 1, 1),)
                    + tuple(shape[a] for a in "yzx")
                    + (tok_rows, cols // PARTS),
                    jnp.bfloat16,
                )
            )
    n = 3 * dp_count + voc_count + size["z"] + size["x"]
    n += HALVES * (size["z"] + 2 * size["x"] + 2 * size["y"])
    n += PARTS * sum(size[a] for a in "yzx")
    loads = -(-main // BLOCK) + 1
    vmem = pl.BlockSpec(memory_space=pltpu.VMEM)
    hbm = pl.BlockSpec(memory_space=pl.ANY)
    dma = pltpu.SemaphoreType.DMA
    return pl.pallas_call(
        functools.partial(head_kernel, grid, voc_cols),
        name="head_step",
        out_shape=[
            jax.ShapeDtypeStruct((8, total_rows), jnp.float32),
            jax.ShapeDtypeStruct(sent.shape, jnp.bfloat16),
        ],
        in_specs=[hbm, hbm] + [vmem] * 5,
        out_specs=[vmem, vmem],
        scratch_shapes=[
            pltpu.VMEM((padded, depth), jnp.bfloat16),
            pltpu.VMEM(x_shape, jnp.bfloat16),
            pltpu.VMEM((depth, total_rows), jnp.bfloat16),
            pltpu.VMEM((padded, total_rows), jnp.float32),
            pltpu.VMEM((total_rows, padded), jnp.bfloat16),
            pltpu.VMEM(part, jnp.float32),
            pltpu.VMEM(part, jnp.float32),
            pltpu.VMEM(part, jnp.float32),
            pltpu.VMEM(part, jnp.bfloat16),
            pltpu.VMEM(sent.shape, jnp.bfloat16),
            pltpu.VMEM(sent.shape, jnp.bfloat16),
            pltpu.VMEM((size["z"], size["x"]) + ids.shape, ids.dtype),
            pltpu.VMEM((voc_count, 8, total_rows), jnp.float32),
            pltpu.VMEM((dp_count, 8, total_rows), jnp.float32),
            dma((loads,)),
            dma((n,)),
            dma((n,)),
            dma((PARTS,)),
            dma((PARTS,)),
        ]
        + recvs,
        compiler_params=pltpu.CompilerParams(
            collective_id=0, has_side_effects=True, vmem_limit_bytes=62 << 20
        ),
        cost_estimate=pl.CostEstimate(
            flops=4 * total_rows * depth * voc_cols,
            bytes_accessed=2 * depth * voc_cols,
            transcendentals=2 * total_rows * voc_cols,
        ),
    )(head, tail, sent, placing, placing_back, cotangent[:, None], ids)


def per_device(hidden, output_head_matrix, row_counts, token_ids, segment_ids, cotangent):
    dp_count = lax.axis_size("dp")
    voc_count = lax.axis_size("vocab")
    dp_index = lax.axis_index("dp")
    grid = Grid(dp_count, voc_count)
    slot_rows, feat_cols = hidden.shape
    per_peer = slot_rows // dp_count
    tok_rows = token_ids.shape[0]
    total_rows = tok_rows * dp_count
    voc_cols = output_head_matrix.shape[1]
    groups = max(1, 16 // per_peer)
    group_cols = feat_cols // groups
    ends = jnp.cumsum(row_counts)
    starts = ends - row_counts
    my_start = starts[dp_index]
    live = jnp.arange(slot_rows, dtype=jnp.int32) < row_counts[dp_index]
    outgoing = jnp.where(live[:, None], hidden, jnp.zeros_like(hidden))
    outgoing = jnp.roll(outgoing.reshape(per_peer, dp_count, feat_cols), my_start, axis=1)
    outgoing = outgoing.reshape(per_peer, dp_count, groups, group_cols)
    outgoing = outgoing.transpose(1, 2, 0, 3).reshape(dp_count, groups * per_peer, group_cols)
    offsets = jnp.mod(dp_index - starts, dp_count)
    base_pos = (starts + offsets - dp_index) // dp_count
    turns = jnp.arange(per_peer, dtype=jnp.int32)[None, :]
    valid = turns * dp_count + offsets[:, None] < row_counts[:, None]
    target = jnp.where(valid, base_pos[:, None] + turns, -1)
    group = jnp.arange(groups, dtype=jnp.int32)
    target = jnp.where(
        (group[:, None] == group[None, :])[:, None, :, None], target[None, :, None, :], -1
    ).reshape(groups, dp_count * groups * per_peer)
    tok = jnp.arange(tok_rows, dtype=jnp.int32)
    placing = (target[:, None, :] == tok[None, :, None]).astype(jnp.bfloat16)
    placing_back = (target[:, :, None] == tok[None, None, :]).astype(jnp.bfloat16)
    own_ids = lax.dynamic_update_slice(
        jnp.zeros((8, total_rows), jnp.int32),
        jnp.stack([token_ids, segment_ids]),
        (0, dp_index * tok_rows),
    )
    all_logprobs, returned = head_step(
        grid, output_head_matrix.T, outgoing, placing, placing_back, cotangent, own_ids, total_rows
    )
    logprobs = lax.dynamic_slice_in_dim(all_logprobs[0], dp_index * tok_rows, tok_rows, 0)
    returned = returned.reshape(dp_count, groups, per_peer, group_cols)
    returned = returned.transpose(2, 0, 1, 3).reshape(per_peer, dp_count, feat_cols)
    grad_hidden = jnp.roll(returned, -my_start, axis=1).reshape(slot_rows, feat_cols)
    return (logprobs, grad_hidden)


def solution(mesh):
    return jax.shard_map(
        per_device,
        mesh=mesh,
        in_specs=(P("dp", "vocab"), P(None, ("dp", "vocab")), P(), P("dp"), P("dp"), P("dp")),
        out_specs=(P("dp"), P("dp", "vocab")),
        check_vma=False,
    )
```

time: 130 us -> 109 us (0.84)
  Pallas kernels: 111 us -> 89.9 us
    pallas_call x5 -> x1, Pallas kernels: 111 us -> 89.9 us  [head_step(): pl.pallas_call(functools.partial(head_kernel, grid, voc_cols), name='head...]
    unnamed x10 -> x2, local copies, waits for them, and re-layouts: 5.4 us -> 0.01 us
where the time goes in v3:
time: 109 us
  Pallas kernels  89.9 us (82%)
  local copies, waits for them, and re-layouts  8.99 us (8%)
  other arithmetic  6.78 us (6%)
  between operations  3.34 us (3%)
    pallas_call x1, Pallas kernels, head_step(): pl.pallas_call(functools.partial(head_kernel, grid, voc_cols), name='head...  89.9 us

profile of v3, /device:TPU:0, one launch (start us, length us, event | category | flops | bytes accessed | tf_op | source)
XLA Modules:
  0.0 109.0 jit_solution(3402249042412389953)
XLA Ops:
  0.6 1.2 %dynamic_slice.14 = s32[1]{0:T(128)} dynamic-slice(s32[8]{0:T(128)} %param.10, s32[]{:T(128)S(6)} %select_n.53), dynamic_slice_sizes={1} | dynamic-slice | bytes 12 | tf_op jit(solution)/shard_map/dynamic_slice | solution.py:505
  1.9 0.6 iota_compare_fusion.3
  2.5 0.8 reduce-window.9
  3.4 0.7 pad_add_fusion
  4.1 0.7 and_select_fusion
  4.7 0.6 dynamic_slice.15
  7.9 0.7 add_select_fusion
  8.7 0.1 broadcast_in_dim.64
  8.8 0.1 broadcast_in_dim.60
  8.8 0.1 broadcast_in_dim.61
  9.0 0.4 dynamic_update_slice.3.ids_ref
  9.4 0.0 copy-start
  9.4 0.6 fusion.4.placing_ref
  10.0 1.3 %copy.10.cot_ref = f32[32,1]{1,0:T(8,128)} copy(f32[32,1]{0,1:T(1,128)} %bitcast.29) | data formatting | bytes 256 | tf_op jit(solution)/shard_map/broadcast_in_dim | solution.py:487
  11.3 0.7 fusion.3.back_ref
  12.0 1.0 select_bitcast_fusion
  13.0 0.1 fusion.2
  13.2 0.1 reshape.158
  13.2 0.7 copy.15
  14.0 0.9 slice.8
  14.9 1.1 pad.4.tail_ref
  16.0 0.0 copy-done
  16.0 89.9 %head_step.1 = (f32[8,256]{1,0:T(8,128)}, bf16[8,16,512]{2,1,0:T(8,128)(2,1)}) custom-call(bf16[4748,4096]{1,0:T(8,128)(2,1)} %bitcast.33, bf16[128,4096]{1,0:T(8,128)(2,1)} %pad.4.tail_ref, bf16[8,16,512]{2,1,0:T(8,128)(2,1)} %bitcast.27, bf16[2,32,128]{2,1,0:T(8,128)(2,1)} %fusion.4.placing_ref, bf16[2,128,32]{2,1,0:T(8,128)(2,1)} %fusion.3.back_ref, ...), custom_call_target="tpu_custom_call" | custom-call | flops 19914555392 | bytes 38895616 | tf_op jit(solution)/shard_map/head_step/pallas_call | solution.py:448
  105.9 0.7 slice.7
  106.6 0.6 fusion.5
  107.2 1.0 copy.14
  108.2 0.1 reshape.161
  108.3 0.8 fusion.1
  (4 shorter events, 0.0 us)
Async XLA Ops:
  9.4 6.6 %copy-start = (s32[8,256]{1,0:T(8,128)}, s32[8,256]{1,0:T(8,128)S(1)}, u32[]{:S(2)}) copy-start(s32[8,256]{1,0:T(8,128)S(1)} %dynamic_update_slice.3.ids_ref) | copy-start | bytes 24580

commit v4 on v3

--- a/solution.py
+++ b/solution.py
@@ -167,7 +167,7 @@
 
 
 def scatter(
-    grid, me, sender, core, cot_ref, placing_ref, out_ref, core_recv, acc, sendbuf, outgoing, recvs
+    grid, me, sender, keep_part, core, cot_ref, placing_ref, out_ref, core_recv, acc, sendbuf, outgoing, recvs
 ):
     dp = lax.axis_index("dp")
 
@@ -187,6 +187,7 @@
         for h in range(PARTS):
             order = SCATTER_ORDERS[h]
             if s == 0:
+                keep_part(h)
                 core(h).wait()
                 acc[h] = acc[h] + core_recv[h]
             else:
@@ -208,7 +209,7 @@
                     )
                 )
     summed = jnp.concatenate([acc[h, me["y"], me["z"], me["x"]] for h in range(PARTS)], axis=1)
-    scaled = (summed * cot_ref[...]).astype(jnp.bfloat16)
+    scaled = (summed * cot_ref[:, 0:1]).astype(jnp.bfloat16)
     group_cols = outgoing.shape[-1]
     slots = sum(
         jnp.dot(
@@ -392,16 +393,15 @@
         core_copy(h).start()
         return carry
 
-    def keep_part(h, carry):
+    def keep_part(h):
         backward_part(h, me["c"], acc)
-        return carry
 
     lax.fori_loop(0, PARTS, send_part, 0)
-    lax.fori_loop(0, PARTS, keep_part, 0)
     scatter(
         grid,
         me,
         sender,
+        keep_part,
         core_copy,
         cot_ref,
         back_ref,
@@ -484,7 +484,7 @@
             bytes_accessed=2 * depth * voc_cols,
             transcendentals=2 * total_rows * voc_cols,
         ),
-    )(head, tail, sent, placing, placing_back, cotangent[:, None], ids)
+    )(head, tail, sent, placing, placing_back, jnp.broadcast_to(cotangent[:, None], (tok_rows, 128)), ids)
 
 
 def per_device(hidden, output_head_matrix, row_counts, token_ids, segment_ids, cotangent):
@@ -499,10 +499,11 @@
     voc_cols = output_head_matrix.shape[1]
     groups = max(1, 16 // per_peer)
     group_cols = feat_cols // groups
-    ends = jnp.cumsum(row_counts)
-    starts = ends - row_counts
-    my_start = starts[dp_index]
-    live = jnp.arange(slot_rows, dtype=jnp.int32) < row_counts[dp_index]
+    device = jnp.arange(dp_count, dtype=jnp.int32)
+    starts = jnp.sum(jnp.where(device[None, :] < device[:, None], row_counts[None, :], 0), axis=1)
+    my_start = jnp.sum(jnp.where(device < dp_index, row_counts, 0))
+    my_count = jnp.sum(jnp.where(device == dp_index, row_counts, 0))
+    live = jnp.arange(slot_rows, dtype=jnp.int32) < my_count
     outgoing = jnp.where(live[:, None], hidden, jnp.zeros_like(hidden))
     outgoing = jnp.roll(outgoing.reshape(per_peer, dp_count, feat_cols), my_start, axis=1)
     outgoing = outgoing.reshape(per_peer, dp_count, groups, group_cols)

time: 109 us -> 104 us (0.954)
  Pallas kernels: 89.9 us -> 86.2 us
  local copies, waits for them, and re-layouts: 8.99 us -> 7.14 us
    pallas_call x1, Pallas kernels: 89.9 us -> 86.2 us  [head_step(): pl.pallas_call(functools.partial(head_kernel, grid, voc_cols), name='head...]
    dynamic_slice x2 -> x0, local copies, waits for them, and re-layouts: 1.83 us -> none  [the longest x1 1.24 us: per_device(): live = jnp.arange(slot_rows, dtype=jnp.int32) < row_counts[dp_index]]
where the time goes in v4:
time: 104 us
  Pallas kernels  86.2 us (83%)
  other arithmetic  7.36 us (7%)
  local copies, waits for them, and re-layouts  7.14 us (7%)
  between operations  3.35 us (3%)
    pallas_call x1, Pallas kernels, head_step(): pl.pallas_call(functools.partial(head_kernel, grid, voc_cols), name='head...  86.2 us

profile of v4, /device:TPU:0, one launch (start us, length us, event | category | flops | bytes accessed | tf_op | source)
XLA Modules:
  0.0 104.0 jit_solution(11579215295007127878)
XLA Ops:
  0.6 0.8 select_reduce_fusion
  1.4 0.7 pad_add_fusion
  2.1 1.3 %and_select_fusion = (s32[8]{0:T(128)S(1)}, s32[8]{0:T(128)S(1)}, s32[]{:T(128)}, s32[]{:T(128)}) fusion(s32[8]{0:T(128)S(1)} %select_reduce_fusion, s32[]{:T(128)S(6)} %axis_index.15, s32[8]{0:T(128)} %param.10), kind=kLoop, calls=%fused_computation.20 | loop fusion | flops 278 | bytes 140 | tf_op jit(solution)/shard_map/jit(floor_divide)/jit(_where)/select_n | solution.py:512
  6.0 0.7 iota_compare_fusion.4
  6.7 0.7 add_select_fusion
  7.4 0.1 broadcast_in_dim.90
  7.5 0.1 broadcast_in_dim.84
  7.6 0.1 broadcast_in_dim.85
  7.7 0.4 dynamic_update_slice.3.ids_ref
  8.1 0.0 copy-start
  8.1 0.6 fusion.4.placing_ref
  8.7 1.3 %broadcast_in_dim.93.cot_ref = f32[32,128]{1,0:T(8,128)} broadcast(f32[32]{0:T(128)} %param.13), dimensions={0} | broadcast | bytes 16512 | tf_op jit(solution)/shard_map/broadcast_in_dim | solution.py:487
  10.0 0.7 fusion.3.back_ref
  10.8 1.0 select_bitcast_fusion
  11.8 0.1 fusion.2
  11.9 0.1 reshape.165
  12.0 0.7 copy.15
  12.7 0.9 slice.8
  13.6 1.1 %pad.4.tail_ref = bf16[128,4096]{1,0:T(8,128)(2,1)} pad(bf16[12,4096]{1,0:T(8,128)(2,1)S(1)} %slice.8, bf16[]{:T(256)} %constant.52.clone.1), padding=0_116x0_0 | pad | bytes 1146882 | tf_op jit(solution)/shard_map/jit(_pad)/pad | solution.py:425
  14.7 0.0 copy-done
  14.7 86.2 %head_step.1 = (f32[8,256]{1,0:T(8,128)}, bf16[8,16,512]{2,1,0:T(8,128)(2,1)}) custom-call(bf16[4748,4096]{1,0:T(8,128)(2,1)} %bitcast.24, bf16[128,4096]{1,0:T(8,128)(2,1)} %pad.4.tail_ref, bf16[8,16,512]{2,1,0:T(8,128)(2,1)} %bitcast.20, bf16[2,32,128]{2,1,0:T(8,128)(2,1)} %fusion.4.placing_ref, bf16[2,128,32]{2,1,0:T(8,128)(2,1)} %fusion.3.back_ref, ...), custom_call_target="tpu_custom_call" | custom-call | flops 19914555392 | bytes 38895616 | tf_op jit(solution)/shard_map/head_step/pallas_call | solution.py:448
  100.9 0.7 slice.7
  101.6 0.6 fusion.5
  102.2 1.0 copy.14
  103.2 0.1 reshape.168
  103.3 0.8 fusion.1
  (5 shorter events, 0.0 us)
Async XLA Ops:
  8.1 6.6 %copy-start = (s32[8,256]{1,0:T(8,128)}, s32[8,256]{1,0:T(8,128)S(1)}, u32[]{:S(2)}) copy-start(s32[8,256]{1,0:T(8,128)S(1)} %dynamic_update_slice.3.ids_ref) | copy-start | bytes 24580
